TPU v7x, 32 devices: a whole 2x2x4 slice. The times are simulated.
32 devices in a mesh: dp: 16 (over z, y, core), tm: 2 (over x).
Axes of the slice: x: 2, y: 2, z: 4, core: 2. Of those that a mesh axis runs over, the one named last changes fastest.
Arguments:
- hidden_in: bfloat16 [2, 16, 512, 1024], P(None, 'dp', 'tm'), may hold values from -6 to 6
- memory: bfloat16 [2, 16, 512, 1024], P(None, 'dp', 'tm'), may hold values from -6 to 6
- compressed_in: bfloat16 [2, 16, 512, 1024], P(None, 'dp', 'tm'), may hold values from -6 to 6
- lengths: int32 [2, 16], P(None, 'dp'), may hold values from 128 to 512, as said below
- gain_attn: bfloat16 [1024], P(('dp', 'tm')), may hold values from 0.099609375 to 1.8984375
- gain_ffn: bfloat16 [1024], P(('dp', 'tm')), may hold values from 0.099609375 to 1.8984375
- w_query: bfloat16 [1024, 1024], P(None, ('dp', 'tm')), may hold values from -0.1875 to 0.1875
- w_key: bfloat16 [1024, 1024], P(None, ('dp', 'tm')), may hold values from -0.1875 to 0.1875
- w_value: bfloat16 [1024, 1024], P(None, ('dp', 'tm')), may hold values from -0.1875 to 0.1875
- w_out: bfloat16 [1024, 1024], P(None, ('dp', 'tm')), may hold values from -4 to 4
- w_up: bfloat16 [1024, 4096], P(None, ('dp', 'tm')), may hold values from -0.1875 to 0.1875
- w_down: bfloat16 [4096, 1024], P(None, ('dp', 'tm')), may hold values from -0.125 to 0.125
- w_compress: bfloat16 [2048, 1024], P(None, ('dp', 'tm')), may hold values from -0.125 to 0.125
- cot_out: bfloat16 [2, 16, 512, 1024], P(None, 'dp', 'tm'), may hold values from -6 to 6
- cot_comp: bfloat16 [2, 16, 256, 1024], P(None, 'dp', 'tm'), may hold values from -6 to 6
Outputs:
- layer_out: bfloat16 [2, 16, 512, 1024], P(None, 'dp', 'tm')
- compressed: bfloat16 [2, 16, 256, 1024], P(None, 'dp', 'tm')
- grad_in: bfloat16 [2, 16, 512, 1024], P(None, 'dp', 'tm')
- grad_gain_attn: float32 [1024], P(('dp', 'tm'))
- grad_gain_ffn: float32 [1024], P(('dp', 'tm'))
- grad_query: float32 [1024, 1024], P(None, ('dp', 'tm'))
- grad_key: float32 [1024, 1024], P(None, ('dp', 'tm'))
- grad_value: float32 [1024, 1024], P(None, ('dp', 'tm'))
- grad_out: float32 [1024, 1024], P(None, ('dp', 'tm'))
- grad_up: float32 [1024, 4096], P(None, ('dp', 'tm'))
- grad_down: float32 [4096, 1024], P(None, ('dp', 'tm'))
- grad_compress: float32 [2048, 1024], P(None, ('dp', 'tm'))
Inputs may be any that keep to these rules, and one draw needn't show every extreme that they name: `lengths`: each length is a quarter of 512, half of 512 or 512. In each micro-batch at least one stream has length 512.
All inputs are finite; a program needn't handle non-finite values.
Results may differ from a plain program's by a relative error of at most 0.014.
Values may be sent and summed in bfloat16 or wider, within the bound.
No kernel may reach another device: no remote copies, remote signals or barrier semaphores. Data moves between devices by JAX's collectives and lax.ppermute only.
A program may use at most 256 MiB of HBM per device.

v0:
```python
import functools
import math

import jax
import jax.numpy as jnp
import numpy as np
from jax import lax
from jax.experimental import pallas as pl
from jax.experimental.pallas import tpu as pltpu
from jax.sharding import PartitionSpec as P

H = 8
DH = 128
MEM = 512
CMEM = 512
COMP = 2

EPSILON = 1e-05
ROPE_BASE = 10000.0
NEG_LARGE = -1e30
SCALE = 1.0 / math.sqrt(DH)
BOTH = ("dp", "tm")
LOW = jnp.bfloat16
F32 = jnp.float32


VMEM = 60 * 2**20
TOGETHER = 2
SMALL = 16 * 2**20
LONG = pl.CostEstimate(flops=10**11, bytes_accessed=2**20, transcendentals=0)


def bit_of(bit):
    return (lax.axis_index("dp") * lax.axis_size("tm") + lax.axis_index("tm")) >> bit & 1


def swap(value, bit):
    count = lax.axis_size(BOTH)
    return lax.ppermute(value, BOTH, [(i, i ^ (1 << bit)) for i in range(count)])


def bit_count():
    return lax.axis_size(BOTH).bit_length() - 1


def ordered_call(kernel, args, waits, in_specs, **settings):
    count, more = len(args), len(waits)

    def body(*refs):
        kernel(*refs[:count], *refs[count + more :])

    return pl.pallas_call(
        body,
        in_specs=list(in_specs) + [pl.BlockSpec(memory_space=pl.ANY)] * more,
        cost_estimate=LONG,
        **settings,
    )(*args, *waits)


def gate_kernel(value, out):
    pass


def gate(value, *waits):
    anywhere = pl.BlockSpec(memory_space=pl.ANY)
    return ordered_call(
        gate_kernel,
        (value,),
        waits,
        [anywhere],
        out_specs=anywhere,
        out_shape=jax.ShapeDtypeStruct(value.shape, value.dtype),
        input_output_aliases={0: 0},
        compiler_params=pltpu.CompilerParams(vmem_limit_bytes=VMEM),
        name="gate",
    )


def copy_kernel(value, out):
    out[...] = value[...]


def copied(value, waits):
    block = pl.BlockSpec(value.shape, lambda i: (0,) * value.ndim)
    return ordered_call(
        copy_kernel,
        (value,),
        waits,
        [block],
        grid=(1,),
        out_specs=block,
        out_shape=jax.ShapeDtypeStruct(value.shape, value.dtype),
        compiler_params=pltpu.CompilerParams(vmem_limit_bytes=VMEM),
        name="copied",
    )


def merge_kernel(mine, own, other, out):
    out[:, mine[0]] = own[...]
    out[:, 1 - mine[0]] = other[...]


def merged(own, other, mine, before, waits):
    width = own.shape[-1]
    own, other = own.reshape(before, -1, width), other.reshape(before, -1, width)
    rest = own.shape[1]
    each = max(1, min(before, 2**18 // (rest * width)))
    block = pl.BlockSpec((each, rest, width), lambda i: (i, 0, 0))
    return ordered_call(
        merge_kernel,
        (mine.reshape(1), own, other),
        waits,
        [pl.BlockSpec(memory_space=pltpu.SMEM), block, block],
        grid=(before // each,),
        out_specs=pl.BlockSpec((each, 2, rest, width), lambda i: (i, 0, 0, 0)),
        out_shape=jax.ShapeDtypeStruct((before, 2, rest, width), own.dtype),
        compiler_params=pltpu.CompilerParams(vmem_limit_bytes=VMEM),
        name="merge",
    )


class Gathering:
    def __init__(self, shard, order):
        self.held, self.order, self.done = shard, list(order), []
        self.lead, self.width = shard.shape[0], shard.shape[-1]
        self.other = swap(shard, order[0])

    def step(self, *waits):
        bit = self.order.pop(0)
        before = self.lead * 2 ** sum(1 for d in self.done if d > bit)
        self.held = merged(self.held, self.other, bit_of(bit), before, waits).reshape(
            self.lead, -1, self.width
        )
        self.done.append(bit)
        if self.order:
            self.other = swap(self.held, self.order[0])
        return self.held


def combine_kernel(count, mine, *refs):
    refs, out = refs[:count], refs[-1]
    total = sum(ref[...].reshape(out.shape).astype(F32) for ref in refs)
    out[...] = total.astype(out.dtype)


def combine_both_kernel(count, axis, bit, mine, *refs):
    refs, (send, kept) = refs[:count], refs[-2:]
    shape = kept.shape[:axis] + (2,) + kept.shape[axis:]
    total = sum(ref[...].reshape(shape).astype(F32) for ref in refs)
    zero, one = (lax.index_in_dim(total, i, axis, keepdims=False) for i in range(2))
    first = mine[bit] == 0
    send[...] = jnp.where(first, one, zero).astype(LOW)
    kept[...] = jnp.where(first, zero, one)


def combined(terms, rest, bit, done, free, waits, both=False):
    whole, size = [], math.prod(rest)
    for b in reversed(free):
        if size < 2**18:
            whole, size = whole + [b], size * 2
    stepped = [b for b in free if b not in whole]

    def spec(bits):
        def index(g, mine):
            place = []
            for b in bits:
                if b == bit:
                    place.append(0 if both else 1 - mine[b])
                elif b in done:
                    place.append(mine[b])
                elif b in whole:
                    place.append(0)
                else:
                    place.append(g >> (len(stepped) - 1 - stepped.index(b)) & 1)
            return tuple(place) + (0,) * len(rest)

        dims = tuple(2 if b in whole or (both and b == bit) else 1 for b in bits)
        return pl.BlockSpec(dims + rest, index)

    out = jax.ShapeDtypeStruct((2,) * len(free) + rest, F32 if bit is None else LOW)
    if both:
        axis = sum(1 for b in free if b > bit)
        kernel = lambda *refs: combine_both_kernel(len(terms), axis, bit, *refs)
        outs, out_specs = [out, jax.ShapeDtypeStruct(out.shape, F32)], [spec(free)] * 2
    else:
        kernel = lambda *refs: combine_kernel(len(terms), *refs)
        outs, out_specs = out, spec(free)
    large = sum(term.size for term, _ in terms) > 2**21
    return pl.pallas_call(
        kernel,
        grid_spec=pltpu.PrefetchScalarGridSpec(
            num_scalar_prefetch=1,
            grid=(2 ** len(stepped),),
            in_specs=[spec(bits) for _, bits in terms]
            + [pl.BlockSpec(memory_space=pl.ANY)] * len(waits),
            out_specs=out_specs,
        ),
        out_shape=outs,
        compiler_params=pltpu.CompilerParams(vmem_limit_bytes=VMEM if large else SMALL),
        cost_estimate=LONG,
        name="combine",
    )(jnp.stack([bit_of(b) for b in range(bit_count())]), *[term for term, _ in terms], *waits)


def round_kernel(plans, mine, *refs):
    ins, outs = refs[: sum(plan[0] for plan in plans)], refs[-sum(1 + plan[3] for plan in plans) :]
    at, out_at = 0, 0
    for count, axis, bit, both in plans:
        terms, at = ins[at : at + count], at + count
        if both:
            send, kept = outs[out_at : out_at + 2]
            combine_both_kernel(count, axis, bit, mine, *terms, send, kept)
        else:
            combine_kernel(count, mine, *terms, outs[out_at])
        out_at += 1 + both


def round_of(chains, waits):
    in_specs, out_specs, outs, args, plans = [], [], [], [], []
    for chain in chains:
        bit = chain.order.pop(0) if chain.order else None
        free = [b for b in chain.bits if b != bit]
        both = bit is not None and len(chain.done) > 1

        def spec(bits, bit=bit, free=free, both=both, done=tuple(chain.done), rest=chain.rest):
            def index(g, mine):
                place = [
                    (0 if both else 1 - mine[b]) if b == bit else mine[b] if b in done else 0
                    for b in bits
                ]
                return tuple(place) + (0,) * len(rest)

            dims = tuple(2 if b in free or (both and b == bit) else 1 for b in bits)
            return pl.BlockSpec(dims + rest, index)

        for term, bits in chain.terms:
            args.append(term)
            in_specs.append(spec(bits))
        shape = (2,) * len(free) + chain.rest
        outs.append(jax.ShapeDtypeStruct(shape, F32 if bit is None else LOW))
        outs.extend([jax.ShapeDtypeStruct(shape, F32)] * both)
        out_specs.extend([spec(free)] * (1 + both))
        axis = sum(1 for b in free if bit is not None and b > bit)
        plans.append((len(chain.terms), axis, bit, both))
    results = list(
        pl.pallas_call(
            lambda *refs: round_kernel(plans, *refs),
            grid_spec=pltpu.PrefetchScalarGridSpec(
                num_scalar_prefetch=1,
                grid=(1,),
                in_specs=in_specs + [pl.BlockSpec(memory_space=pl.ANY)] * len(waits),
                out_specs=out_specs,
            ),
            out_shape=outs,
            compiler_params=pltpu.CompilerParams(vmem_limit_bytes=VMEM),
            cost_estimate=LONG,
            name="round",
        )(jnp.stack([bit_of(b) for b in range(bit_count())]), *args, *waits)
    )
    last = results[0]
    for chain, (_, _, bit, both) in zip(chains, plans):
        send = results.pop(0)
        if bit is None:
            chain.total = send
            continue
        chain.bits = [b for b in chain.bits if b != bit]
        if both:
            chain.terms = [(results.pop(0), chain.bits)]
        chain.done.append(bit)
        chain.terms.append((swap(send, bit), chain.bits))
    return last


class Chain:
    def __init__(self, keep, send, order, rest):
        self.bits = [b for b in range(bit_count() - 1, -1, -1) if b != 1]
        self.rest = rest
        shape = (2,) * len(self.bits) + rest
        self.terms = [
            (keep.reshape(shape), self.bits),
            (swap(send.reshape(shape), 1), self.bits),
        ]
        self.order, self.done = list(order), [1]

    def step(self, *waits):
        bit = self.order.pop(0)
        self.bits = [b for b in self.bits if b != bit]
        both = len(self.done) > 1
        send = combined(self.terms, self.rest, bit, self.done, self.bits, waits, both)
        if both:
            send, kept = send
            self.terms = [(kept, self.bits)]
        self.done.append(bit)
        self.terms.append((swap(send, bit), self.bits))
        return send

    def finish(self, *waits):
        return combined(self.terms, self.rest, None, self.done, [], waits)


def gather_order(last):
    high = list(range(bit_count() - 1, 2, -1))
    return {"y": high + [0, 2, 1], "x": high + [2, 0, 1], "x_first": [0] + high + [2, 1]}[last]


def gather(shard, order):
    held, done = shard, []
    for bit in order:
        other = swap(held, bit)
        mine = bit_of(bit) == 1
        axis = 1 + sum(1 for d in done if d > bit)
        held = jnp.stack(
            [jnp.where(mine, other, held), jnp.where(mine, held, other)], axis=axis
        )
        done.append(bit)
    return held.reshape(shard.shape[0], -1, shard.shape[2])


def scatter(whole, order, kept=LOW):
    count = lax.axis_size(BOTH)
    bits = bit_count()
    held = whole.reshape((2,) * bits + (whole.shape[0] // count, whole.shape[1]))
    left = list(range(bits))
    for bit in order:
        axis = sum(1 for d in left if d > bit)
        mine = bit_of(bit)
        other = swap(lax.dynamic_index_in_dim(held, 1 - mine, axis, keepdims=False), bit)
        keep = lax.dynamic_index_in_dim(held, mine, axis, keepdims=False)
        left.remove(bit)
        held = keep.astype(F32) + other.astype(F32)
        if left:
            held = held.astype(kept)
    return held


def scatter_order(first):
    high = list(range(3, bit_count()))
    return {"y": [1, 2, 0] + high, "x": [1, 0, 2] + high}[first]


def norm_parts(values):
    centre = values - jnp.mean(values, axis=-1, keepdims=True)
    spread = jnp.mean(centre * centre, axis=-1, keepdims=True)
    rate = lax.rsqrt(spread + EPSILON)
    return centre * rate, rate


def norm_back(grad, unit, rate, gain):
    scaled = grad * gain
    return rate * (
        scaled
        - jnp.mean(scaled, axis=-1, keepdims=True)
        - unit * jnp.mean(scaled * unit, axis=-1, keepdims=True)
    )


def turn_tables(positions):
    half = DH // 2
    frequency = jnp.exp(jnp.arange(half, dtype=F32) * (-2.0 * math.log(ROPE_BASE) / DH))
    angles = positions.astype(F32)[:, None] * frequency[None, :]
    cosine, sine = jnp.cos(angles), jnp.sin(angles)
    return (
        jnp.concatenate([cosine, cosine], axis=1),
        jnp.concatenate([-sine, sine], axis=1),
    )


def turned(values, cosine, sine):
    return values * cosine + pltpu.roll(values, DH // 2, 1) * sine


def unturned(values, cosine, sine):
    return values * cosine - pltpu.roll(values, DH // 2, 1) * sine


def dot_nt(left, right):
    return lax.dot_general(left, right, (((1,), (1,)), ((), ())), preferred_element_type=F32)


def dot_nn(left, right):
    return lax.dot_general(left, right, (((1,), (0,)), ((), ())), preferred_element_type=F32)


def dot_tn(left, right):
    return lax.dot_general(left, right, (((0,), (0,)), ((), ())), preferred_element_type=F32)


def attend_kernel(late, query, ka, kb, va, vb, context, pa_out, pb_out):
    rows = query.shape[0]
    base = SCALE * math.log2(math.e)
    sides = ((ka, va, pa_out), (kb, vb, pb_out))
    for head in range(query.shape[1] // DH):
        lanes = slice(head * DH, (head + 1) * DH)
        scores = []
        for side, (key, _, _) in enumerate(sides):
            for part in range(3):
                score = dot_nt(key[part, :, lanes], query[:, lanes])
                if part == 2:
                    key_at = lax.broadcasted_iota(jnp.int32, (rows, rows), 0)
                    if side == 0:
                        seen = key_at <= lax.broadcasted_iota(jnp.int32, (rows, rows), 1)
                    else:
                        seen = key_at < late[0] * rows
                    score = jnp.where(seen, score, NEG_LARGE)
                scores.append(score)
        top = functools.reduce(jnp.maximum, scores)
        top = jnp.max(top, axis=0, keepdims=True) * base
        exps = [jnp.exp2(score * base - top) for score in scores]
        total = jnp.sum(sum(exps), axis=0, keepdims=True)
        share = 1.0 / total
        mixed = 0.0
        for i, value in enumerate(exps):
            attn = (value * share).astype(LOW)
            side, part = divmod(i, 3)
            sides[side][2][0, head, part * rows : (part + 1) * rows, :] = attn
            mixed += dot_tn(sides[side][1][part, :, lanes], attn)
        context[:, lanes] = mixed.T.astype(LOW)


def attend_back_kernel(
    grad, query, ka, kb, va, vb, pa, pb, cos_a, sin_a, cos_b, sin_b,
    gq_out, gka_out, gkb_out, gva_out, gvb_out,
):
    rows = query.shape[0]
    lead = 2 * rows
    sides = (
        (ka, va, pa, cos_a, sin_a, gka_out, gva_out),
        (kb, vb, pb, cos_b, sin_b, gkb_out, gvb_out),
    )
    for head in range(query.shape[1] // DH):
        lanes = slice(head * DH, (head + 1) * DH)
        here, own = grad[:, lanes], query[:, lanes]
        backs, inner = [], 0.0
        for _, value, attn, _, _, _, out in sides:
            for part in range(3):
                weights = attn[0, head, part * rows : (part + 1) * rows, :]
                back = dot_nt(value[part, :, lanes], here)
                inner += weights.astype(F32) * back
                out[part, :, lanes] = dot_nn(weights, here).astype(LOW)
                backs.append(back)
        inner = jnp.sum(inner, axis=0, keepdims=True)
        mixed = 0.0
        for i, back in enumerate(backs):
            side, part = divmod(i, 3)
            key, _, attn, cosine, sine, out, _ = sides[side]
            at = slice(part * rows, (part + 1) * rows)
            score = (attn[0, head, at, :].astype(F32) * (back - inner)).astype(LOW)
            grads = dot_nn(score, own) * SCALE
            out[part, :, lanes] = unturned(grads, cosine[at, :], sine[at, :]).astype(LOW)
            mixed += dot_tn(key[part, :, lanes], score)
        gq_out[:, lanes] = unturned(mixed.T * SCALE, cos_a[lead:, :], sin_a[lead:, :]).astype(LOW)


def feed_kernel(
    mine, ffn, grad, up_a_own, up_a_far, up_b_own, up_b_far,
    down_p_own, down_p_far, down_q_own, down_q_far,
    branch, grad_ffn, up_keep, up_send, down_keep, down_send, ffn_t, grad_t, up_nat, down_nat,
):
    half = up_a_own.shape[1]
    core, across = mine[0], mine[2]
    own_at = pl.multiple_of(core * half, half)
    far_at = pl.multiple_of((1 - core) * half, half)
    step = pl.program_id(0)
    first = step == 0
    group, _, _, each, _ = down_nat.shape

    @pl.when(first)
    def _():
        ffn_t[...] = ffn[...].T
        grad_t[...] = grad[...].T.reshape(grad_t.shape)

    for place, (own, far) in enumerate(((up_a_own, up_a_far), (up_b_own, up_b_far))):

        @pl.when(step % 2 == place)
        def _():
            up_nat[:half] = own[0]
            up_nat[half:] = far[0]

    for ref, at_core, at in (
        (down_p_own, core, across),
        (down_p_far, 1 - core, across),
        (down_q_own, core, 1 - across),
        (down_q_far, 1 - core, 1 - across),
    ):
        down_nat[:, at_core, at, :, :half] = ref[:, pl.ds(own_at, half)].reshape(group, each, half)
        down_nat[:, at_core, at, :, half:] = ref[:, pl.ds(far_at, half)].reshape(group, each, half)
    up_rows = up_nat[...]
    down_rows = down_nat[...].reshape(-1, 2 * half)
    upper = dot_nt(ffn[...], up_rows)
    slope = math.sqrt(2.0 / math.pi)
    square = upper * upper
    bent = jnp.tanh(slope * upper * (1.0 + 0.044715 * square))
    share = 0.5 + 0.5 * bent
    active = (upper * share).astype(LOW)
    gelu_slope = share + 0.5 * upper * (1.0 - bent * bent) * (
        slope + (3.0 * 0.044715 * slope) * square
    )
    grad_hidden = (dot_nn(grad[...], down_rows) * gelu_slope).astype(LOW)
    more_out = dot_nt(active, down_rows)
    more_grad = dot_nn(grad_hidden, up_rows)

    @pl.when(first)
    def _():
        branch[...] = more_out
        grad_ffn[...] = more_grad

    @pl.when(jnp.logical_not(first))
    def _():
        branch[...] += more_out
        grad_ffn[...] += more_grad

    for ref, at in ((up_keep, 0), (up_send, half)):
        part = dot_nn(ffn_t[...], grad_hidden[:, at : at + half]).astype(LOW)
        ref[0, 0] = part[:, : half // 2]
        ref[0, 1] = part[:, half // 2 :]
    for ref, at in ((down_keep, core), (down_send, 1 - core)):
        part = dot_nn(grad_t[:, at].reshape(group * 2 * each, -1), active).astype(LOW)
        ref[:, pl.ds(own_at, half)] = part[:, :half]
        ref[:, pl.ds(far_at, half)] = part[:, half:]


def feed_forward(mine, ffn, grad_branch, up_parts, down_parts):
    rows, width = ffn.shape
    groups, half = up_parts[0].shape[:2]
    steps, wide = 2 * groups, 2 * half

    def whole(*dims):
        return pl.BlockSpec(dims, lambda t, m: (0,) * len(dims))

    def place(t, m):
        return t // 2 * 2 + (m[1] + t) % 2

    shape = jax.ShapeDtypeStruct
    up_in = pl.BlockSpec((1, half, width), lambda t, m: (t // 2, 0, 0))
    up_out = pl.BlockSpec((1, 2, width, half // 2), lambda t, m: (place(t, m), 0, 0, 0))

    def lanes(count):
        return pl.BlockSpec((count, wide), lambda t, m: (0, place(t, m)))

    return pl.pallas_call(
        feed_kernel,
        grid_spec=pltpu.PrefetchScalarGridSpec(
            num_scalar_prefetch=1,
            grid=(steps,),
            in_specs=[whole(rows, width)] * 2 + [up_in] * 4 + [lanes(width // 4)] * 4,
            out_specs=[whole(rows, width)] * 2 + [up_out] * 2 + [lanes(width // 2)] * 2,
            scratch_shapes=[
                pltpu.VMEM((width, rows), LOW),
                pltpu.VMEM((steps, 2, width // 2 // steps, rows), LOW),
                pltpu.VMEM((wide, width), LOW),
                pltpu.VMEM((steps, 2, 2, width // 4 // steps, wide), LOW),
            ],
        ),
        out_shape=[shape((rows, width), F32)] * 2
        + [shape((steps, 2, width, half // 2), LOW)] * 2
        + [shape((width // 2, steps * wide), LOW)] * 2,
        compiler_params=pltpu.CompilerParams(vmem_limit_bytes=VMEM),
        cost_estimate=LONG,
        name="feed_forward",
    )(mine, ffn, grad_branch, *up_parts, *down_parts)


def norm_kernel(hidden, gain, normed, even, odd, wide):
    rows, width = hidden.shape
    unit, _ = norm_parts(hidden[...].astype(F32))
    normed[...] = (unit * gain[...]).astype(LOW)
    for i in range(width // DH):
        lanes = slice(i * DH, (i + 1) * DH)
        wide[i] = normed[:, lanes].astype(F32)
        even[:, lanes] = wide[i, pl.ds(0, rows // 2, 2), :].astype(LOW)
        odd[:, lanes] = wide[i, pl.ds(1, rows // 2, 2), :].astype(LOW)


def norm_rows(hidden, gain, waits=()):
    rows, width = hidden.shape
    some = rows // 2
    block, half = rows_spec(some, width), rows_spec(some // 2, width)
    shape = jax.ShapeDtypeStruct
    return ordered_call(
        norm_kernel,
        (hidden, gain,),
        waits,
        [block, whole_spec(1, width)],
        grid=(2,),
        out_specs=[block, half, half],
        out_shape=[shape((rows, width), LOW)] + [shape((rows // 2, width), LOW)] * 2,
        scratch_shapes=[pltpu.VMEM((width // DH, some, DH), F32)],
        compiler_params=pltpu.CompilerParams(vmem_limit_bytes=VMEM),
        name="norm_rows",
    )


def project_kernel(own, cmem, mem, normed, weight, cosine, sine, key, value, *query):
    rows, width = cmem.shape
    which, segment = pl.program_id(0), pl.program_id(1)
    times = rows // cosine.shape[1]

    def product(source):
        return dot_nt(source[...], weight[...].reshape(width, width))

    def turned_product(source, out):
        lin = product(source)
        cos = jnp.concatenate([cosine[0]] * times, axis=0)
        sin = jnp.concatenate([sine[0]] * times, axis=0)
        for head in range(width // DH):
            lanes = slice(head * DH, (head + 1) * DH)
            out[:, lanes] = turned(lin[:, lanes], cos, sin).astype(LOW)

    for i, source in enumerate((cmem, mem, normed)):

        @pl.when((segment == i) & (which == 0))
        def _():
            turned_product(source, key.at[0])

        @pl.when((segment == i) & (which == 1))
        def _():
            value[0] = product(source).astype(LOW)

    if own:

        @pl.when((segment == 2) & (which == 2))
        def _():
            turned_product(normed, query[0])


def project(cmem, mem, normed, weights, tables, own, waits=()):
    rows, width = normed.shape
    count, _, unit, _ = weights.shape
    per = width // count // unit
    shape = jax.ShapeDtypeStruct
    whole = pl.BlockSpec((rows, width), lambda w, i: (0, 0))
    tables = [table.reshape(3, -1, DH) for table in tables]
    table = pl.BlockSpec((1,) + tables[0].shape[1:], lambda w, i: (jnp.where(w < 2, i, 2), 0, 0))
    outs = [
        pl.BlockSpec((1, rows, width), lambda w, i: (jnp.where(w == 0, i, 2), 0, 0)),
        pl.BlockSpec(
            (1, rows, width),
            lambda w, i: (jnp.where(w == 0, 0, jnp.where(w == 1, i, 2)), 0, 0),
        ),
    ]
    return ordered_call(
        lambda *refs: project_kernel(own, *refs),
        (cmem, mem, normed, weights, *tables,),
        waits,
        [whole] * 3
        + [pl.BlockSpec((count, per, unit, width), lambda w, i: (0, w, 0, 0))]
        + [table] * 2,
        grid=(3 if own else 2, 3),
        out_specs=outs + [whole] * own,
        out_shape=[shape((3, rows, width), LOW)] * 2 + [shape((rows, width), LOW)] * own,
        compiler_params=pltpu.CompilerParams(vmem_limit_bytes=VMEM),
        name="project",
    )


def weight_grads_kernel(counts, each, core, *refs):
    total_count = sum(counts)
    grads, sources = refs[:total_count], refs[total_count : 2 * total_count]
    *extra, keep, send = refs[2 * total_count :]
    first, at = core[0] == 0, 0
    groups, depth = keep.shape[0], keep.shape[-1]
    for place, count in enumerate(counts):
        total = sum(dot_tn(grads[i][0], sources[i][...]) for i in range(at, at + count))
        at += count
        total = total.astype(LOW).reshape(groups, 2, 2, each, depth)
        rows = slice(place * each, (place + 1) * each)
        keep[:, :, rows] = jnp.where(first, total[:, 0], total[:, 1])
        send[:, :, rows] = jnp.where(first, total[:, 1], total[:, 0])
    if extra:
        rows = slice(len(counts) * each, None)
        keep[:, :, rows] = extra[0][...]
        send[:, :, rows] = extra[1][...]


def weight_grads(core, problems, each, waits=(), extra=()):
    pairs = [pair for problem in problems for pair in problem]
    grads = [g if isinstance(g, tuple) else (g[None], 0) for g, _ in pairs]
    sources = [source for _, source in pairs]
    width, depth = grads[0][0].shape[2], sources[0].shape[1]
    groups = 4
    wide = groups * 4 * each
    more = extra[0].shape[2] if extra else 0

    def spec(array, place):
        return pl.BlockSpec((1, array.shape[1], wide), lambda i: (place, 0, i))

    out = (groups, 2, len(problems) * each + more, depth)
    return ordered_call(
        lambda *refs: weight_grads_kernel([len(p) for p in problems], each, *refs),
        (core.reshape(1), *[array for array, _ in grads], *sources, *extra),
        waits,
        [pl.BlockSpec(memory_space=pltpu.SMEM)]
        + [spec(array, place) for array, place in grads]
        + [whole_spec(*source.shape) for source in sources]
        + [pl.BlockSpec((groups, 2, more, depth), lambda i: (i, 0, 0, 0))] * len(extra),
        grid=(width // wide,),
        out_specs=[pl.BlockSpec(out, lambda i: (i, 0, 0, 0))] * 2,
        out_shape=[jax.ShapeDtypeStruct((width // (4 * each),) + out[1:], LOW)] * 2,
        compiler_params=pltpu.CompilerParams(vmem_limit_bytes=VMEM),
        name="weight_grads",
    )


def weight_spec(weights, which):
    count, _, unit, width = weights.shape
    per = width // count // unit
    return pl.BlockSpec((count, per, unit, width), lambda i: (0, which, 0, 0))


def rows_spec(rows, width):
    return pl.BlockSpec((rows, width), lambda i: (i, 0))


def whole_spec(*dims):
    return pl.BlockSpec(dims, lambda i: (0,) * len(dims))


def far_kernel(late, grad_key, grad_value, comp, w_key, w_value, w_before, out):
    rows, width = out.shape
    total = dot_nn(grad_key[0], w_key[...].reshape(width, width))
    total += dot_nn(grad_value[0], w_value[...].reshape(width, width))
    rim = dot_nn(comp[0, :16], w_before[...].reshape(width, width))[:1] * late[0].astype(F32)
    last = lax.broadcasted_iota(jnp.int32, (rows, width), 0) == rows - 1
    out[...] = (total + jnp.where(last, rim, 0.0)).astype(LOW)


def far_back(late, grad_keys, grad_values, comp_grad, weights, later, waits=()):
    batch, _, width = comp_grad.shape
    rows = grad_keys.shape[1] // batch
    last_part = pl.BlockSpec((1, rows, width), lambda i: (2, i, 0))
    return ordered_call(
        far_kernel,
        (late.reshape(1), grad_keys, grad_values, comp_grad, weights, weights, later,),
        waits,
        [pl.BlockSpec(memory_space=pltpu.SMEM), last_part, last_part]
        + [pl.BlockSpec((1,) + comp_grad.shape[1:], lambda i: (i, 0, 0))]
        + [weight_spec(weights, 0), weight_spec(weights, 1), weight_spec(later, 0)],
        grid=(batch,),
        out_specs=rows_spec(rows, width),
        out_shape=jax.ShapeDtypeStruct((batch * rows, width), LOW),
        compiler_params=pltpu.CompilerParams(vmem_limit_bytes=VMEM),
        name="far_back",
    )


def finish_kernel(
    grad_query, grad_key, grad_value, comp, token, hidden, grad_middle, gain,
    w_query, w_key, w_value, w_before, w_at, grad_in, grad_gain, wide,
):
    rows, width = hidden.shape
    half = rows // 2
    before = dot_nn(comp[0], w_before[...].reshape(width, width))
    before = jnp.where(
        lax.broadcasted_iota(jnp.int32, (half, width), 0) == half - 1,
        0.0,
        pltpu.roll(before, half - 1, 0),
    )
    at = dot_nn(comp[0], w_at[...].reshape(width, width))
    for i in range(width // DH):
        lanes = slice(i * DH, (i + 1) * DH)
        wide[i, pl.ds(0, half, 2), :] = at[:, lanes]
        wide[i, pl.ds(1, half, 2), :] = before[:, lanes]
    grads = jnp.concatenate([wide[i] for i in range(width // DH)], axis=1)
    grads += token[...].astype(F32)
    for left, weight in ((grad_query, w_query), (grad_key, w_key), (grad_value, w_value)):
        grads += dot_nn(left[...].reshape(rows, width), weight[...].reshape(width, width))
    unit, rate = norm_parts(hidden[...].astype(F32))
    total = jnp.sum(grads * unit, axis=0, keepdims=True)
    grad_in[...] = (grad_middle[...] + norm_back(grads, unit, rate, gain[...])).astype(LOW)
    first = pl.program_id(0) == 0

    @pl.when(first)
    def _():
        grad_gain[...] = total

    @pl.when(jnp.logical_not(first))
    def _():
        grad_gain[...] += total


def finish(
    grad_query, grad_keys, grad_values, comp_grad, token, hidden, grad_middle, gain, weights, later, waits=()):
    batch = comp_grad.shape[0]
    rows, width = hidden.shape
    some = rows // batch
    block = rows_spec(some, width)
    last_part = pl.BlockSpec((1, some, width), lambda i: (2, i, 0))
    shape = jax.ShapeDtypeStruct
    return ordered_call(
        finish_kernel,
        (grad_query, grad_keys, grad_values, comp_grad, token, hidden, grad_middle, gain,
        weights, weights, weights, later, later,),
        waits,
        [block, last_part, last_part]
        + [pl.BlockSpec((1,) + comp_grad.shape[1:], lambda i: (i, 0, 0))]
        + [block] * 3
        + [whole_spec(1, width)]
        + [weight_spec(weights, which) for which in (2, 0, 1)]
        + [weight_spec(later, which) for which in (0, 1)],
        grid=(batch,),
        out_specs=[block, whole_spec(1, width)],
        out_shape=[shape((rows, width), LOW), shape((1, width), F32)],
        scratch_shapes=[pltpu.VMEM((width // DH, some, DH), F32)],
        compiler_params=pltpu.CompilerParams(vmem_limit_bytes=VMEM),
        name="finish",
    )


def outputs_kernel(before, at, mask, middle, branch, live, w_before, w_at, compressed, layer_out):
    width = compressed.shape[1]
    total = dot_nt(before[...], w_before[...].reshape(width, width))
    total += dot_nt(at[...], w_at[...].reshape(width, width))
    compressed[...] = (total * mask[...]).astype(LOW)
    layer_out[...] = ((middle[...] + branch[...]) * live[...]).astype(LOW)


def outputs(before, at, mask, middle, branch, live, later, waits=()):
    rows, width = middle.shape
    some, few = rows // 2, at.shape[0] // 2
    shape = jax.ShapeDtypeStruct
    return ordered_call(
        outputs_kernel,
        (before, at, mask, middle, branch, live, later, later),
        waits,
        [rows_spec(few, width), rows_spec(few, width), rows_spec(few, 1)]
        + [rows_spec(some, width), rows_spec(some, width), rows_spec(some, 1)]
        + [weight_spec(later, which) for which in (0, 1)],
        grid=(2,),
        out_specs=[rows_spec(few, width), rows_spec(some, width)],
        out_shape=[shape(at.shape, LOW), shape((rows, width), LOW)],
        compiler_params=pltpu.CompilerParams(vmem_limit_bytes=VMEM),
        name="outputs",
    )


def join_kernel(context, hidden, gain, weight, middle, ffn):
    width = middle.shape[1]
    middle[...] = hidden[...].astype(F32) + dot_nt(
        context[...], weight[...].reshape(width, width)
    )
    unit, _ = norm_parts(middle[...])
    ffn[...] = (unit * gain[...]).astype(LOW)


def join(context, hidden, gain, weights, waits=()):
    rows, width = hidden.shape
    some = rows // 2
    block = rows_spec(some, width)
    shape = jax.ShapeDtypeStruct
    return ordered_call(
        join_kernel,
        (context, hidden, gain, weights,),
        waits,
        [block, block, whole_spec(1, width), weight_spec(weights, 0)],
        grid=(2,),
        out_specs=[block, block],
        out_shape=[shape((rows, width), F32), shape((rows, width), LOW)],
        compiler_params=pltpu.CompilerParams(vmem_limit_bytes=VMEM),
        name="join",
    )


def part_kernel(
    grad_ffn, middle, cot, live, gain, weight, grad_middle, grad_low, grad_context, grad_gain
):
    width = middle.shape[1]
    unit, rate = norm_parts(middle[...])
    grads = grad_ffn[...]
    grad_middle[...] = cot[...].astype(F32) * live[...] + norm_back(
        grads, unit, rate, gain[...]
    )
    grad_low[...] = grad_middle[...].astype(LOW)
    grad_context[...] = dot_nn(grad_low[...], weight[...].reshape(width, width)).astype(LOW)
    total = jnp.sum(grads * unit, axis=0, keepdims=True)
    first = pl.program_id(0) == 0

    @pl.when(first)
    def _():
        grad_gain[...] = total

    @pl.when(jnp.logical_not(first))
    def _():
        grad_gain[...] += total


def part(grad_ffn, middle, cot, live, gain, weights, waits=()):
    rows, width = middle.shape
    some = rows // 2
    block = rows_spec(some, width)
    shape = jax.ShapeDtypeStruct
    return ordered_call(
        part_kernel,
        (grad_ffn, middle, cot, live, gain, weights,),
        waits,
        [block] * 3
        + [rows_spec(some, 1), whole_spec(1, width), weight_spec(weights, 0)],
        grid=(2,),
        out_specs=[block] * 3 + [whole_spec(1, width)],
        out_shape=[
            shape((rows, width), F32),
            shape((rows, width), LOW),
            shape((rows, width), LOW),
            shape((1, width), F32),
        ],
        compiler_params=pltpu.CompilerParams(vmem_limit_bytes=VMEM),
        name="part",
    )


def head_spec(rows):
    return pl.BlockSpec((rows, TOGETHER * DH), lambda b, h: (b, h))


def keys_spec(rows):
    return pl.BlockSpec((3, rows, TOGETHER * DH), lambda b, h: (0, b, h))


def table_spec(rows):
    return pl.BlockSpec((rows, DH), lambda b, h: (0, 0))


def attn_spec(keys, rows):
    return pl.BlockSpec((1, TOGETHER, keys, rows), lambda b, h: (b, h, 0, 0))


def attend(late, query, ka, kb, va, vb, batch, waits=()):
    rows, width = query.shape[0] // batch, query.shape[1]
    keys = 3 * rows
    shape = jax.ShapeDtypeStruct
    return ordered_call(
        attend_kernel,
        (late, query, ka, kb, va, vb,),
        waits,
        [pl.BlockSpec(memory_space=pltpu.SMEM), head_spec(rows)] + [keys_spec(rows)] * 4,
        grid=(batch, H // TOGETHER),
        out_specs=[head_spec(rows)] + [attn_spec(keys, rows)] * 2,
        out_shape=[shape((batch * rows, width), LOW)]
        + [shape((batch, H, keys, rows), LOW)] * 2,
        compiler_params=pltpu.CompilerParams(vmem_limit_bytes=VMEM),
        name="attend",
    )


def attend_back(grad, query, ka, kb, va, vb, pa, pb, tables, batch, waits=()):
    rows, width = query.shape[0] // batch, query.shape[1]
    keys = 3 * rows
    shape = jax.ShapeDtypeStruct
    return ordered_call(
        attend_back_kernel,
        (grad, query, ka, kb, va, vb, pa, pb, *tables,),
        waits,
        [head_spec(rows)] * 2
        + [keys_spec(rows)] * 4
        + [attn_spec(keys, rows)] * 2
        + [table_spec(keys)] * 4,
        grid=(batch, H // TOGETHER),
        out_specs=[head_spec(rows)] + [keys_spec(rows)] * 4,
        out_shape=[shape((batch * rows, width), LOW)]
        + [shape((3, batch * rows, width), LOW)] * 4,
        compiler_params=pltpu.CompilerParams(vmem_limit_bytes=VMEM),
        name="attend_back",
    )


def local_general(
    hidden_in, memory, compressed_in, lengths, gain_attn, gain_ffn,
    w_query, w_key, w_value, w_out, w_up, w_down, w_compress, cot_out, cot_comp,
):
    micro, streams, block, width = hidden_in.shape
    batch = micro * streams
    rows = batch * block
    late = lax.axis_index("tm")
    windows_each = block // COMP

    hidden = hidden_in.reshape(batch, block, width)
    mem = memory.reshape(batch, -1, width)
    cmem = compressed_in.reshape(batch, -1, width)
    hidden_far = swap(hidden, 0)
    mem_far = swap(mem, 0)
    cmem_far = swap(cmem, 0)

    gains = gather(
        jnp.stack([gain_attn, gain_ffn]).reshape(2, 1, -1), gather_order("x_first")
    ).reshape(2, width).astype(F32)
    gain_first, gain_second = gains[0], gains[1]
    key_value = gather(jnp.stack([w_key.T, w_value.T]), gather_order("x_first"))
    query_out = gather(jnp.stack([w_query.T, w_out.T]), gather_order("x_first"))
    up_t = gather(w_up.T[None], gather_order("x"))[0]
    down_t = gather(w_down.T[None], gather_order("y"))[0]
    compress_t = gather(w_compress.T[None], gather_order("y"))[0]
    key_t, value_t = key_value[0], key_value[1]
    query_t, out_t = query_out[0], query_out[1]

    cmem_size, mem_size = cmem.shape[1], mem.shape[1]

    def positions(half):
        return jnp.concatenate(
            [
                COMP * (half * cmem_size + jnp.arange(cmem_size, dtype=jnp.int32) - CMEM) - MEM,
                half * mem_size + jnp.arange(mem_size, dtype=jnp.int32) - MEM,
                half * block + jnp.arange(block, dtype=jnp.int32),
            ]
        )

    tables = turn_tables(positions(late)) + turn_tables(positions(1 - late))
    lens = lengths.reshape(batch)
    query_pos = late * block + jnp.arange(block, dtype=jnp.int32)
    window_end = late * block + COMP * jnp.arange(windows_each, dtype=jnp.int32)
    row_mask = (query_pos[None, :] < lens[:, None]).astype(F32)[..., None]
    window_mask = (window_end[None, :] < lens[:, None]).astype(F32)[..., None]

    inputs = hidden.astype(F32)
    unit, rate = norm_parts(inputs)
    normed = (unit * gain_first).astype(LOW)
    unit_far, _ = norm_parts(hidden_far.astype(F32))
    normed_far = (unit_far * gain_first).astype(LOW)

    rim = normed_far[:, block - 1 :] * (late == 1).astype(LOW)
    padded = jnp.concatenate([rim, normed[:, : block - 1]], axis=1)
    windows = padded.reshape(batch * windows_each, COMP * width)
    comp_grad = (
        (cot_comp.reshape(batch, windows_each, width).astype(F32) * window_mask)
        .astype(LOW)
        .reshape(batch * windows_each, width)
    )
    compressed = dot_nt(windows, compress_t).reshape(batch, windows_each, width) * window_mask
    grad_compress = scatter(dot_tn(comp_grad, windows).astype(LOW), scatter_order("y"))
    grad_windows = dot_nn(comp_grad, compress_t).reshape(batch, block, width)
    rim_grad = swap(grad_windows[:, :1].astype(LOW), 0).astype(F32) * (late == 0).astype(F32)
    grad_shifted = jnp.concatenate([grad_windows[:, 1:], rim_grad], axis=1)

    near = jnp.stack([cmem, mem, normed]).reshape(-1, width)
    far = jnp.stack([cmem_far, mem_far, normed_far]).reshape(-1, width)
    normed = normed.reshape(rows, width)

    def by_head(lin, cosine, sine):
        shape = (-1, batch, block, H, DH)
        cosine, sine = (table.reshape(-1, 1, block, 1, DH) for table in (cosine, sine))
        lin = lin.reshape(shape)
        turn = lin * cosine + jnp.roll(lin, DH // 2, axis=-1) * sine
        return turn.astype(LOW).reshape(-1, rows, width)

    query = by_head(dot_nt(normed, query_t), tables[0][-block:], tables[1][-block:])[0]
    ka = by_head(dot_nt(near, key_t), *tables[:2])
    kb = by_head(dot_nt(far, key_t), *tables[2:])
    va, vb = (
        dot_nt(part, value_t).astype(LOW).reshape(3, rows, width) for part in (near, far)
    )
    context, pa, pb = attend(late.reshape(1), query, ka, kb, va, vb, batch)
    middle = inputs.reshape(rows, width) + dot_nt(context, out_t)

    unit_ffn, rate_ffn = norm_parts(middle)
    ffn = (unit_ffn * gain_second).astype(LOW)
    upper = dot_nt(ffn, up_t)
    slope = math.sqrt(2.0 / math.pi)
    bent = jnp.tanh(slope * (upper + 0.044715 * upper * upper * upper))
    active = (0.5 * upper * (1.0 + bent)).astype(LOW)
    gelu_slope = 0.5 * (1.0 + bent) + 0.5 * upper * (1.0 - bent * bent) * slope * (
        1.0 + 3.0 * 0.044715 * upper * upper
    )
    branch = dot_nt(active, down_t)
    live = row_mask.reshape(rows, 1)
    layer_out = ((middle + branch) * live).astype(LOW)
    grad_live = cot_out.reshape(rows, width).astype(F32) * live
    grad_branch = grad_live.astype(LOW)
    grad_upper = (dot_nn(grad_branch, down_t) * gelu_slope).astype(LOW)
    grad_down = scatter(dot_tn(grad_branch, active).astype(LOW), scatter_order("y"))
    grad_up = scatter(dot_tn(grad_upper, ffn).astype(LOW), scatter_order("x"))
    grad_ffn = dot_nn(grad_upper, up_t)
    grad_gain_ffn = jnp.sum(grad_ffn * unit_ffn, axis=0)
    grad_middle = grad_live + norm_back(grad_ffn, unit_ffn, rate_ffn, gain_second)

    grad_attended = grad_middle.astype(LOW)
    grad_out = scatter(dot_tn(grad_attended, context).astype(LOW), scatter_order("y"))
    grad_context = dot_nn(grad_attended, out_t).astype(LOW)
    gq, *parts = attend_back(grad_context, query, ka, kb, va, vb, pa, pb, tables, batch)
    gka, gkb, gva, gvb = (part.reshape(-1, width) for part in parts)
    grad_value = scatter(
        (dot_tn(gva, near) + dot_tn(gvb, far)).astype(LOW), scatter_order("x")
    )
    grad_key = scatter((dot_tn(gka, near) + dot_tn(gkb, far)).astype(LOW), scatter_order("y"))
    grad_query = scatter(dot_tn(gq, normed).astype(LOW), scatter_order("x"))

    def token_rows(values):
        return values[-rows:]

    token_far = dot_nn(token_rows(gkb), key_t) + dot_nn(token_rows(gvb), value_t)
    token_back = swap(token_far.astype(LOW), 0).astype(F32)
    grad_normed = (
        dot_nn(gq, query_t)
        + dot_nn(token_rows(gka), key_t)
        + dot_nn(token_rows(gva), value_t)
        + grad_shifted.reshape(rows, width)
        + token_back
    )
    unit = unit.reshape(rows, width)
    grad_gain_attn = jnp.sum(grad_normed * unit, axis=0)
    grad_in = grad_middle + norm_back(grad_normed, unit, rate.reshape(rows, 1), gain_first)
    gain_grads = scatter(
        jnp.stack([grad_gain_attn, grad_gain_ffn], axis=1), scatter_order("x"), F32
    )

    return (
        layer_out.reshape(hidden_in.shape),
        compressed.astype(LOW).reshape(cot_comp.shape),
        grad_in.astype(LOW).reshape(hidden_in.shape),
        gain_grads[:, 0],
        gain_grads[:, 1],
        grad_query.T,
        grad_key.T,
        grad_value.T,
        grad_out.T,
        grad_up.T,
        grad_down.T,
        grad_compress.T,
    )


def local(
    hidden_in, memory, compressed_in, lengths, gain_attn, gain_ffn,
    w_query, w_key, w_value, w_out, w_up, w_down, w_compress, cot_out, cot_comp,
):
    count = lax.axis_size(BOTH)
    micro, streams, block, width = hidden_in.shape
    unit_rows, hidden_rows = width // count, w_up.shape[1]
    if unit_rows % 32 or hidden_rows % 128:
        return local_general(
            hidden_in, memory, compressed_in, lengths, gain_attn, gain_ffn,
            w_query, w_key, w_value, w_out, w_up, w_down, w_compress, cot_out, cot_comp,
        )
    batch = micro * streams
    rows = batch * block
    late, core = lax.axis_index("tm"), bit_of(1)
    windows_each = block // COMP
    hidden = hidden_in.reshape(batch, block, width)
    mem = memory.reshape(batch, -1, width)
    cmem = compressed_in.reshape(batch, -1, width)
    high = list(range(bit_count() - 1, 2, -1))
    early = [0] + high + [2, 1]

    half_unit = unit_rows // 2

    def gathered_groups(parts, *waits):
        shard = jnp.concatenate(parts).reshape(1, -1, half_unit, width)
        shard = copied(shard, waits) if waits else shard
        return shard, lax.all_gather(shard, BOTH, axis=0, tiled=True)

    gain_rows = jnp.zeros((half_unit, width), LOW)
    gain_rows = gain_rows.at[0, : 2 * unit_rows].set(jnp.concatenate([gain_attn, gain_ffn]))
    _, attention_in = gathered_groups([w_key.T, w_value.T, w_query.T, gain_rows])
    _, out_in = gathered_groups([w_out.T])
    hidden, mem, cmem = (part.reshape(rows, width) for part in (hidden, mem, cmem))
    up_in = Gathering(w_up.T[None], [0] + high + [2])
    down_in = Gathering(w_down.T[None], high + [2, 0])
    hidden_far, cmem_far, mem_far = (swap(part, 0) for part in (hidden, cmem, mem))

    positions = np.concatenate(
        [
            COMP * (np.arange(CMEM) - CMEM) - MEM,
            np.arange(MEM) - MEM,
            np.arange(2 * block),
        ]
    ).astype(np.float32)
    frequency = np.exp(
        np.arange(DH // 2, dtype=np.float32) * np.float32(-2.0 * math.log(ROPE_BASE) / DH)
    ).astype(np.float32)
    angles = positions[:, None] * frequency[None, :]
    turns = np.stack(
        [
            np.concatenate([np.cos(angles), np.cos(angles)], axis=1),
            np.concatenate([-np.sin(angles), np.sin(angles)], axis=1),
        ]
    ).astype(np.float32)
    turns = jnp.asarray(turns.reshape(2, 3, 2, -1, DH))

    def tables_of(half):
        return tuple(lax.dynamic_index_in_dim(turns, half, 2, False).reshape(2, -1, DH))

    tables = tables_of(late) + tables_of(1 - late)
    lens = lengths.reshape(batch)
    query_pos = late * block + jnp.arange(block, dtype=jnp.int32)
    window_end = late * block + COMP * jnp.arange(windows_each, dtype=jnp.int32)
    row_mask = (query_pos[None, :] < lens[:, None]).astype(F32)[..., None]
    window_mask = (window_end[None, :] < lens[:, None]).astype(F32)[..., None]
    live = row_mask.reshape(rows, 1)
    grad_live = cot_out.reshape(rows, width).astype(F32) * live
    grad_branch = grad_live.astype(LOW)

    outward = high[::-1]
    last = down_in.step()
    last = up_in.step(last)
    last = down_in.step(last)
    last = up_in.step(last)


    ones = jnp.ones((1, width), F32)
    _, unit_even, unit_odd = norm_rows(hidden, ones, (last,))
    unit_far, _, _ = norm_rows(hidden_far, ones, (unit_even,))

    def rows_before(far_rows, odd_rows):
        far_rows, odd_rows = (value.reshape(batch, -1, width) for value in (far_rows, odd_rows))
        rim = far_rows[:, block - 1 :] * (late == 1).astype(LOW)
        return jnp.concatenate([rim, odd_rows[:, : windows_each - 1]], axis=1).reshape(-1, width)

    comp_grad = (cot_comp.reshape(batch, windows_each, width).astype(F32) * window_mask).astype(LOW)
    comp_rows = comp_grad.reshape(-1, width)
    keep, send = weight_grads(
        core,
        [[(comp_rows, rows_before(unit_far, unit_odd))], [(comp_rows, unit_even)]],
        unit_rows,
    )
    compress_sum = Chain(keep, send, outward + [2, 0], (2 * unit_rows, width))
    last = down_in.step(keep, grad_branch, *tables)
    last = up_in.step(last)
    last = compress_sum.step(last)
    up_held, up_other, down_held, down_other = (
        part.reshape(shape)
        for chain, shape in (
            (up_in, (count // 8, -1, width)),
            (down_in, (-1, hidden_rows * count)),
        )
        for part in (chain.held, chain.other)
    )

    gains = (
        attention_in[:, 6, 0, : 2 * unit_rows]
        .reshape(count, 2, unit_rows)
        .transpose(1, 0, 2)
        .reshape(2, width)
        .astype(F32)
    )
    gain_first, gain_second = gains[:1], gains[1:]
    normed, even, odd = norm_rows(hidden, gain_first, (last,))
    ka, va, query = project(cmem, mem, normed, attention_in, tables[:2], True)
    normed_far, _, _ = norm_rows(hidden_far, gain_first, (query,))
    kb, vb = project(cmem_far, mem_far, normed_far, attention_in, tables[2:], False)

    context, pa, pb = attend(late.reshape(1), query, ka, kb, va, vb, batch)
    last, compress_in = gathered_groups([w_compress[:width].T, w_compress[width:].T], context)
    up_other, down_other = gate(up_other, last), gate(down_other, last)
    up_parts = [up_held, swap(up_held, 1), up_other, swap(up_other, 1)]
    down_parts = [down_held, swap(down_held, 1), down_other, swap(down_other, 1)]
    middle, ffn = join(context, hidden, gain_second, out_in, (last,))

    branch, grad_ffn, up_keep, up_send, down_keep, down_send = feed_forward(
        jnp.stack([core, bit_of(2), late]), ffn, grad_branch, up_parts, down_parts
    )
    up_sum = Chain(up_keep, up_send, [0, 2] + outward, up_keep.shape[2:])
    down_sum = Chain(
        down_keep, down_send, [2, 0] + outward, (unit_rows, hidden_rows * count)
    )

    grad_middle, grad_low, grad_context, grad_gain_ffn = part(
        grad_ffn, middle, cot_out.reshape(rows, width), live, gain_second, out_in
    )
    last = up_sum.step(grad_context)
    last = down_sum.step(last)

    gq, gka, gkb, gva, gvb = attend_back(
        grad_context, query, ka, kb, va, vb, pa, pb, tables, batch, (last,)
    )
    before = rows_before(normed_far, odd)
    sources = (cmem, mem, normed, cmem_far, mem_far, normed_far)

    def source_problem(near, far):
        grads = [(grad, i) for grad in (near, far) for i in range(3)]
        return list(zip(grads, sources))

    keep, send = weight_grads(
        core, [source_problem(gva, gvb), [(grad_low, context)]], unit_rows
    )
    value_sum = Chain(keep, send, [2, 0] + outward, (2 * unit_rows, width))
    token_far = far_back(late, gkb, gvb, comp_grad, attention_in, compress_in, (keep,))
    token_back = swap(token_far, 0)
    last = up_sum.step(token_far)
    last = down_sum.step(last)
    last = value_sum.step(last)
    keep, send = weight_grads(
        core, [source_problem(gka, gkb), [(gq, normed)]], unit_rows, (last,)
    )
    key_sum = Chain(keep, send, [0, 2] + outward, (2 * unit_rows, width))
    last = up_sum.step(keep)
    last = key_sum.step(last)
    last = compress_sum.step(last)

    grad_in, grad_gain_attn = finish(
        gq, gka, gva, comp_grad, token_back, hidden, grad_middle, gain_first,
        attention_in, compress_in, (last,),
    )
    gain_pair = (
        jnp.concatenate([grad_gain_attn, grad_gain_ffn])
        .reshape(2, -1, 2, 2, unit_rows)
        .transpose(2, 1, 3, 0, 4)
        .reshape(2, -1, 2, 1, 2 * unit_rows)
        .astype(LOW)
    )
    gain_pair = jnp.pad(gain_pair, ((0, 0),) * 3 + ((0, 15), (0, DH - 2 * unit_rows)))
    gain_sum = Chain(
        lax.dynamic_index_in_dim(gain_pair, core, 0, keepdims=False),
        lax.dynamic_index_in_dim(gain_pair, 1 - core, 0, keepdims=False),
        [2, 0] + outward,
        (16, DH),
    )
    last = round_of([value_sum, down_sum, up_sum], (grad_in,))
    last = round_of([key_sum, gain_sum], (last,))
    last = round_of([value_sum, down_sum, compress_sum], (last,))
    last = round_of([key_sum, gain_sum, up_sum], (last,))
    last = round_of([value_sum, compress_sum], (last,))
    last = round_of([key_sum, down_sum, gain_sum], (last,))
    compressed, layer_out = outputs(
        before, even, window_mask.reshape(-1, 1), middle, branch, live, compress_in, (last,)
    )
    last = round_of([value_sum, compress_sum], (compressed,))
    last = round_of([key_sum, gain_sum], (last,))
    round_of([gain_sum], (last,))
    grad_value, grad_out = jnp.split(value_sum.total, 2)
    grad_before, grad_at = jnp.split(compress_sum.total * gain_first, 2)
    gain_grads = gain_sum.total[0, : 2 * unit_rows]
    grad_key, grad_query = jnp.split(key_sum.total, 2)

    return (
        layer_out.reshape(hidden_in.shape),
        compressed.reshape(cot_comp.shape),
        grad_in.reshape(hidden_in.shape),
        gain_grads[:unit_rows],
        gain_grads[unit_rows:],
        grad_query.T,
        grad_key.T,
        grad_value.T,
        grad_out.T,
        up_sum.total,
        down_sum.total.T,
        jnp.concatenate([grad_before.T, grad_at.T]),
    )


def solution(mesh):
    rows = P(None, "dp", "tm", None)
    columns = P(None, BOTH)
    return jax.shard_map(
        local,
        mesh=mesh,
        in_specs=(rows, rows, rows, P(None, "dp"), P(BOTH), P(BOTH))
        + (columns,) * 7
        + (rows, rows),
        out_specs=(rows, rows, rows, P(BOTH), P(BOTH)) + (columns,) * 7,
        check_vma=False,
    )
```

profile of v0, /device:TPU:0, one launch (start us, length us, event | category | flops | bytes accessed | tf_op | source)
XLA Modules:
  0.0 455.1 jit_solution(14506615122239517475)
XLA Ops:
  37.7 25.3 %collective-permute-done.4 = bf16[1,64,4096]{2,1,0:T(8,128)(2,1)S(1)} collective-permute-done((bf16[1,64,4096]{2,1,0:T(8,128)(2,1)}, bf16[1,64,4096]{2,1,0:T(8,128)(2,1)S(1)}, u32[]{:S(2)}, u32[]{:S(2)}) %collective-permute-start.4) | collective-permute-done | bytes 524320 | tf_op jit(solution)/shard_map/ppermute | solution.py:39
  88.3 11.7 %collective-permute-done.7 = bf16[1,128,4096]{2,1,0:T(8,128)(2,1)} collective-permute-done((bf16[1,128,4096]{2,1,0:T(8,128)(2,1)}, bf16[1,128,4096]{2,1,0:T(8,128)(2,1)}, u32[]{:S(2)}, u32[]{:S(2)}) %collective-permute-start.7) | collective-permute-done | bytes 1048608 | tf_op jit(solution)/shard_map/ppermute | solution.py:39
  103.3 5.8 %collective-permute-done.6 = bf16[1,512,1024]{2,1,0:T(8,128)(2,1)} collective-permute-done((bf16[1,512,1024]{2,1,0:T(8,128)(2,1)}, bf16[1,512,1024]{2,1,0:T(8,128)(2,1)}, u32[]{:S(2)}, u32[]{:S(2)}) %collective-permute-start.6) | collective-permute-done | bytes 1048608 | tf_op jit(solution)/shard_map/ppermute | solution.py:39
  123.8 15.6 %project.2 = (bf16[3,512,1024]{2,1,0:T(8,128)(2,1)}, bf16[3,512,1024]{2,1,0:T(8,128)(2,1)}, bf16[512,1024]{1,0:T(8,128)(2,1)}) custom-call(bf16[512,1024]{1,0:T(8,128)(2,1)} %bitcast.193, bf16[512,1024]{1,0:T(8,128)(2,1)} %bitcast.197, bf16[512,1024]{1,0:T(8,128)(2,1)} %get-tuple-element.113.refs_2_.refs_10_.refs_14_, ...), custom_call_target="tpu_custom_call" | custom-call | flops 99999997952 | bytes 1048576 | tf_op jit(solution)/shard_map/project/pallas_call | solution.py:52
  143.0 13.3 %project.3 = (bf16[3,512,1024]{2,1,0:T(8,128)(2,1)}, bf16[3,512,1024]{2,1,0:T(8,128)(2,1)}) custom-call(bf16[512,1024]{1,0:T(8,128)(2,1)} %collective-permute-done.8.refs_0_.refs_11_, bf16[512,1024]{1,0:T(8,128)(2,1)} %collective-permute-done.9.refs_1_.refs_12_, bf16[512,1024]{1,0:T(8,128)(2,1)} %get-tuple-element.115.refs_2_.refs_13_, ...), custom_call_target="tpu_custom_call" | custom-call | flops 99999997952 | bytes 1048576 | tf_op jit(solution)/shard_map/project/pallas_call | solution.py:52
  156.3 19.6 %attend.1 = (bf16[512,1024]{1,0:T(8,128)(2,1)}, bf16[2,8,768,256]{3,2,1,0:T(8,128)(2,1)}, bf16[2,8,768,256]{3,2,1,0:T(8,128)(2,1)}) custom-call(s32[1]{0:T(128)} %bitcast.53.refs_0_, bf16[512,1024]{1,0:T(8,128)(2,1)} %get-tuple-element.114.refs_2_.refs_1_, bf16[3,512,1024]{2,1,0:T(8,128)(2,1)} %get-tuple-element.118.refs_2_, ...), custom_call_target="tpu_custom_call" | custom-call | flops 99999997952 | bytes 1048576 | tf_op jit(solution)/shard_map/attend/pallas_call | solution.py:52
  179.1 5.0 %join.1 = (f32[512,1024]{1,0:T(8,128)}, bf16[512,1024]{1,0:T(8,128)(2,1)}) custom-call(bf16[512,1024]{1,0:T(8,128)(2,1)} %get-tuple-element.122.refs_1_.refs_0_.refs_14_, bf16[512,1024]{1,0:T(8,128)(2,1)} %bitcast.203, f32[1,1024]{1,0:T(1,128)} %slice.76.refs_2_.refs_4_, bf16[32,2,16,1024]{3,2,1,0:T(8,128)(2,1)} %all-gather.6.cloned.1.call-done.refs_3_.refs_5_, ...), custom_call_target="tpu_custom_call" | custom-call | flops 99999997952 | bytes 1048576 | tf_op jit(solution)/shard_map/join/pallas_call | solution.py:52
  187.9 41.2 %feed_forward.1 = (f32[512,1024]{1,0:T(8,128)}, f32[512,1024]{1,0:T(8,128)}, bf16[8,2,1024,128]{3,2,1,0:T(8,128)(2,1)}, bf16[8,2,1024,128]{3,2,1,0:T(8,128)(2,1)...) custom-call(s32[3]{0:T(128)} %pad_add_fusion.mine, bf16[512,1024]{1,0:T(8,128)(2,1)} %get-tuple-element.124.ffn, ...), custom_call_target="tpu_custom_call" | custom-call | flops 99999997952 | bytes 1048576 | tf_op jit(solution)/shard_map/feed_forward/pallas_call | solution.py:540
  229.7 7.4 %part.1 = (f32[512,1024]{1,0:T(8,128)}, bf16[512,1024]{1,0:T(8,128)(2,1)}, bf16[512,1024]{1,0:T(8,128)(2,1)}, f32[1,1024]{1,0:T(1,128)}) custom-call(f32[512,1024]{1,0:T(8,128)} %get-tuple-element.126.refs_0_, f32[512,1024]{1,0:T(8,128)} %get-tuple-element.123.refs_1_.refs_3_, bf16[512,1024]{1,0:T(8,128)(2,1)} %bitcast.150, f32[512,1]{1,0:T(8,128)} %bitcast.164, ...), custom_call_target="tpu_custom_call" | custom-call | flops 99999997952 | bytes 1048576 | tf_op jit(solution)/shard_map/part/pallas_call | solution.py:52
  238.4 5.1 %combine.10.refs_3_ = bf16[2,2,2,1024,128]{4,3,2,1,0:T(8,128)(2,1)} custom-call(s32[5]{0:T(128)} %copy-done, bf16[2,2,2,2,1024,128]{5,4,3,2,1,0:T(8,128)(2,1)} %bitcast.222, bf16[2,2,2,2,1024,128]{5,4,3,2,1,0:T(8,128)(2,1)} %collective-permute-done.17.refs_2_, bf16[512,1024]{1,0:T(8,128)(2,1)} %get-tuple-element.127.refs_3_.refs_0_), custom_call_target="tpu_custom_call" | custom-call | flops 99999997952 | bytes 1048576 | tf_op jit(solution)/shard_map/combine/pallas_call | solution.py:189
  243.4 5.3 %collective-permute-start.20 = (bf16[2,2,2,1024,128]{4,3,2,1,0:T(8,128)(2,1)}, bf16[2,2,2,1024,128]{4,3,2,1,0:T(8,128)(2,1)}, u32[]{:S(2)}, u32[]{:S(2)}) collective-permute-start(bf16[2,2,2,1024,128]{4,3,2,1,0:T(8,128)(2,1)} %combine.10.refs_3_), channel_id=1, source_target_pairs={{0,1},{1,0},{2,3},{3,2},{4,5},{5,4},{6,7},{7,6},{8,9},{9,8},{10,11... | collective-permute-start | bytes 6291464 | tf_op jit(solution)/shard_map/ppermute | solution.py:39
  248.8 5.0 %combine.11.refs_12_ = bf16[2,2,2,32,4096]{4,3,2,1,0:T(8,128)(2,1)} custom-call(s32[5]{0:T(128)} %copy-done, bf16[2,2,2,2,32,4096]{5,4,3,2,1,0:T(8,128)(2,1)} %bitcast.220, bf16[2,2,2,2,32,4096]{5,4,3,2,1,0:T(8,128)(2,1)} %collective-permute-done.16.refs_2_, bf16[2,2,2,1024,128]{4,3,2,1,0:T(8,128)(2,1)} %combine.10.refs_3_), custom_call_target="tpu_custom_call" | custom-call | flops 99999997952 | bytes 1048576 | tf_op jit(solution)/shard_map/combine/pallas_call | solution.py:189
  254.3 23.7 %attend_back.1 = (bf16[512,1024]{1,0:T(8,128)(2,1)}, bf16[3,512,1024]{2,1,0:T(8,128)(2,1)}, bf16[3,512,1024]{2,1,0:T(8,128)(2,1)}, bf16[3,512,1024]{2,1,0:T(8,128)(2,1)}, bf16[3,512,1024]{2,1,0:T(8,128)(2,1)}) custom-call(bf16[512,1024]{1,0:T(8,128)(2,1)} %get-tuple-element.127.refs_3_.refs_0_, bf16[512,1024]{1,0:T(8,128)(2,1)} %get-tuple-element.114.refs_2_.refs_1_, ...), custom_call_target="tpu_custom_call" | custom-call | flops 99999997952 | bytes 1048576 | tf_op jit(solution)/shard_map/attend_back/pallas_call | solution.py:52
  278.0 14.0 %weight_grads.4 = (bf16[8,2,64,1024]{3,2,1,0:T(8,128)(2,1)}, bf16[8,2,64,1024]{3,2,1,0:T(8,128)(2,1)}) custom-call(s32[1]{0:T(128)} %bitcast.10.refs_0_, bf16[3,512,1024]{2,1,0:T(8,128)(2,1)} %get-tuple-element.137.refs_1_.refs_2_.refs_3_, bf16[3,512,1024]{2,1,0:T(8,128)(2,1)} %get-tuple-element.137.refs_1_.refs_2_.refs_3_, ...), custom_call_target="tpu_custom_call" | custom-call | flops 99999997952 | bytes 1048576 | tf_op jit(solution)/shard_map/weight_grads/pallas_call | solution.py:52
  292.1 7.5 %far_back.1.refs_4_ = bf16[512,1024]{1,0:T(8,128)(2,1)} custom-call(s32[1]{0:T(128)} %bitcast.53.refs_0_, bf16[3,512,1024]{2,1,0:T(8,128)(2,1)} %get-tuple-element.135.refs_1_.refs_4_.refs_5_.refs_6_, bf16[3,512,1024]{2,1,0:T(8,128)(2,1)} %get-tuple-element.138.refs_4_.refs_5_.refs_6_.refs_2_, bf16[2,128,1024]{2,1,0:T(8,128)(2,1)} %fusion.refs_3_, ...), custom_call_target="tpu_custom_call" | custom-call | flops 99999997952 | bytes 1048576 | tf_op jit(solution)/shard_map/far_back/pallas_call | solution.py:52
  299.6 5.1 %combine.12 = (bf16[2,2,1024,128]{3,2,1,0:T(8,128)(2,1)}, f32[2,2,1024,128]{3,2,1,0:T(8,128)}) custom-call(s32[5]{0:T(128)} %copy-done, bf16[2,2,2,2,1024,128]{5,4,3,2,1,0:T(8,128)(2,1)} %bitcast.223, bf16[2,2,2,2,1024,128]{5,4,3,2,1,0:T(8,128)(2,1)} %collective-permute-done.17.refs_2_, bf16[2,2,2,1024,128]{4,3,2,1,0:T(8,128)(2,1)} %collective-permute-done.20.refs_3_, ...), custom_call_target="tpu_custom_call" | custom-call | flops 99999997952 | bytes 1048576 | tf_op jit(solution)/shard_map/combine/pallas_call | solution.py:189
  306.3 5.1 %combine.13 = (bf16[2,2,32,4096]{3,2,1,0:T(8,128)(2,1)}, f32[2,2,32,4096]{3,2,1,0:T(8,128)}) custom-call(s32[5]{0:T(128)} %copy-done, bf16[2,2,2,2,32,4096]{5,4,3,2,1,0:T(8,128)(2,1)} %bitcast.221, bf16[2,2,2,2,32,4096]{5,4,3,2,1,0:T(8,128)(2,1)} %collective-permute-done.16.refs_2_, bf16[2,2,2,32,4096]{4,3,2,1,0:T(8,128)(2,1)} %collective-permute-done.19.refs_3_, ...), custom_call_target="tpu_custom_call" | custom-call | flops 99999997952 | bytes 1048576 | tf_op jit(solution)/shard_map/combine/pallas_call | solution.py:189
  318.0 14.7 %weight_grads.5 = (bf16[8,2,64,1024]{3,2,1,0:T(8,128)(2,1)}, bf16[8,2,64,1024]{3,2,1,0:T(8,128)(2,1)}) custom-call(s32[1]{0:T(128)} %bitcast.10.refs_0_, bf16[3,512,1024]{2,1,0:T(8,128)(2,1)} %get-tuple-element.134.refs_1_.refs_2_.refs_3_, bf16[3,512,1024]{2,1,0:T(8,128)(2,1)} %get-tuple-element.134.refs_1_.refs_2_.refs_3_, ...), custom_call_target="tpu_custom_call" | custom-call | flops 99999997952 | bytes 1048576 | tf_op jit(solution)/shard_map/weight_grads/pallas_call | solution.py:52
  349.1 12.0 %finish.1 = (bf16[512,1024]{1,0:T(8,128)(2,1)}, f32[1,1024]{1,0:T(1,128)}) custom-call(bf16[512,1024]{1,0:T(8,128)(2,1)} %get-tuple-element.136.refs_0_, bf16[3,512,1024]{2,1,0:T(8,128)(2,1)} %get-tuple-element.134.refs_1_.refs_2_.refs_3_, bf16[3,512,1024]{2,1,0:T(8,128)(2,1)} %get-tuple-element.137.refs_1_.refs_2_.refs_3_, ...), custom_call_target="tpu_custom_call" | custom-call | flops 99999997952 | bytes 1048576 | tf_op jit(solution)/shard_map/finish/pallas_call | solution.py:52
  362.1 6.3 %round.9 = (bf16[2,2,64,1024]{3,2,1,0:T(8,128)(2,1)}, f32[2,2,64,1024]{3,2,1,0:T(8,128)}, bf16[2,32,4096]{2,1,0:T(8,128)(2,1)}, f32[2,32,4096]{2,1,0:T(8,128)}, ...) custom-call(s32[5]{0:T(128)} %copy-done, bf16[2,2,2,2,64,1024]{5,4,3,2,1,0:T(8,128)(2,1)} %bitcast.146, ...), custom_call_target="tpu_custom_call" | custom-call | flops 99999997952 | bytes 1048576 | tf_op jit(solution)/shard_map/round/pallas_call | solution.py:246
  376.9 6.7 %collective-permute-done.33.refs_2_ = bf16[2,2,64,1024]{3,2,1,0:T(8,128)(2,1)S(1)} collective-permute-done((bf16[2,2,64,1024]{3,2,1,0:T(8,128)(2,1)}, bf16[2,2,64,1024]{3,2,1,0:T(8,128)(2,1)S(1)}, u32[]{:S(2)}, u32[]{:S(2)}) %collective-permute-start.33) | collective-permute-done | bytes 524320 | tf_op jit(solution)/shard_map/ppermute | solution.py:39
  383.8 6.1 %collective-permute-done.34.refs_4_ = bf16[2,32,4096]{2,1,0:T(8,128)(2,1)S(1)} collective-permute-done((bf16[2,32,4096]{2,1,0:T(8,128)(2,1)}, bf16[2,32,4096]{2,1,0:T(8,128)(2,1)S(1)}, u32[]{:S(2)}, u32[]{:S(2)}) %collective-permute-start.34) | collective-permute-done | bytes 524320 | tf_op jit(solution)/shard_map/ppermute | solution.py:39
  404.6 5.4 %collective-permute-done.39.refs_2_ = bf16[2,64,1024]{2,1,0:T(8,128)(2,1)S(1)} collective-permute-done((bf16[2,64,1024]{2,1,0:T(8,128)(2,1)}, bf16[2,64,1024]{2,1,0:T(8,128)(2,1)S(1)}, u32[]{:S(2)}, u32[]{:S(2)}) %collective-permute-start.39) | collective-permute-done | bytes 262176 | tf_op jit(solution)/shard_map/ppermute | solution.py:39
  421.8 7.0 %outputs.1 = (bf16[256,1024]{1,0:T(8,128)(2,1)}, bf16[512,1024]{1,0:T(8,128)(2,1)}) custom-call(bf16[256,1024]{1,0:T(8,128)(2,1)} %bitcast.152, bf16[256,1024]{1,0:T(8,128)(2,1)} %get-tuple-element.117.refs_1_, f32[256,1]{1,0:T(8,128)} %copy.54.refs_2_, f32[512,1024]{1,0:T(8,128)} %get-tuple-element.123.refs_1_.refs_3_, ...), custom_call_target="tpu_custom_call" | custom-call | flops 99999997952 | bytes 1048576 | tf_op jit(solution)/shard_map/outputs/pallas_call | solution.py:52
  (245 shorter events, 166.9 us)
Async XLA Ops:
  7.2 111.2 %all-gather.4.cloned.1.call-start = ((), (), s32[]{:S(2)}) async-start(), calls=%async_computation | async-start | bytes 7569408 | tf_op jit(solution)/shard_map/all_gather | solution.py:1146
  9.7 169.4 %all-gather.6.cloned.1.call-start = ((), (), s32[]{:S(2)}) async-start(), calls=%async_computation.1 | async-start | bytes 2162688 | tf_op jit(solution)/shard_map/all_gather | solution.py:1146
  16.5 62.5 %collective-permute-start = (bf16[512,1024]{1,0:T(8,128)(2,1)}, bf16[512,1024]{1,0:T(8,128)(2,1)}, u32[]{:S(2)}, u32[]{:S(2)}) collective-permute-start(bf16[512,1024]{1,0:T(8,128)(2,1)} %bitcast.200), channel_id=1, source_target_pairs={{0,1},{1,0},{2,3},{3,2},{4,5},{5,4},{6,7},{7,6},{8,9},{9,8},{10,11... | collective-permute-start | bytes 3145736 | tf_op jit(solution)/shard_map/ppermute | solution.py:39
  17.0 125.7 %collective-permute-start.8 = (bf16[512,1024]{1,0:T(8,128)(2,1)}, bf16[512,1024]{1,0:T(8,128)(2,1)}, u32[]{:S(2)}, u32[]{:S(2)}) collective-permute-start(bf16[512,1024]{1,0:T(8,128)(2,1)} %bitcast.192), channel_id=1, source_target_pairs={{0,1},{1,0},{2,3},{3,2},{4,5},{5,4},{6,7},{7,6},{8,9},{9,8},{10,11... | collective-permute-start | bytes 3145736 | tf_op jit(solution)/shard_map/ppermute | solution.py:39
  18.5 124.5 %collective-permute-start.9 = (bf16[512,1024]{1,0:T(8,128)(2,1)}, bf16[512,1024]{1,0:T(8,128)(2,1)}, u32[]{:S(2)}, u32[]{:S(2)}) collective-permute-start(bf16[512,1024]{1,0:T(8,128)(2,1)} %bitcast.196), channel_id=1, source_target_pairs={{0,1},{1,0},{2,3},{3,2},{4,5},{5,4},{6,7},{7,6},{8,9},{9,8},{10,11... | collective-permute-start | bytes 3145736 | tf_op jit(solution)/shard_map/ppermute | solution.py:39
  19.1 273.0 %all-gather.8.cloned.1.call-start = ((), (), s32[]{:S(2)}) async-start(), calls=%async_computation.2 | async-start | bytes 4325376 | tf_op jit(solution)/shard_map/all_gather | solution.py:1146
  34.0 29.0 %collective-permute-start.4 = (bf16[1,64,4096]{2,1,0:T(8,128)(2,1)}, bf16[1,64,4096]{2,1,0:T(8,128)(2,1)S(1)}, u32[]{:S(2)}, u32[]{:S(2)}) collective-permute-start(bf16[1,64,4096]{2,1,0:T(8,128)(2,1)} %bitcast.214), channel_id=1, source_target_pairs={{0,8},{1,9},{2,10},{3,11},{4,12},{5,13},{6,14},{7,15},{8,0},{9,1},... | collective-permute-start | bytes 1572872 | tf_op jit(solution)/shard_map/ppermute | solution.py:39
  37.4 34.3 %collective-permute-start.3 = (bf16[1,256,1024]{2,1,0:T(8,128)(2,1)}, bf16[1,256,1024]{2,1,0:T(8,128)(2,1)S(1)}, u32[]{:S(2)}, u32[]{:S(2)}) collective-permute-start(bf16[1,256,1024]{2,1,0:T(8,128)(2,1)} %bitcast.211), channel_id=1, source_target_pairs={{0,16},{1,17},{2,18},{3,19},{4,20},{5,21},{6,22},{7,23},{8,24},{9,... | collective-permute-start | bytes 1572872 | tf_op jit(solution)/shard_map/ppermute | solution.py:39
  66.0 33.9 %collective-permute-start.7 = (bf16[1,128,4096]{2,1,0:T(8,128)(2,1)}, bf16[1,128,4096]{2,1,0:T(8,128)(2,1)}, u32[]{:S(2)}, u32[]{:S(2)}) collective-permute-start(bf16[1,128,4096]{2,1,0:T(8,128)(2,1)} %bitcast.208), channel_id=1, source_target_pairs={{0,4},{1,5},{2,6},{3,7},{4,0},{5,1},{6,2},{7,3},{8,12},{9,13},{10,... | collective-permute-start | bytes 3145736 | tf_op jit(solution)/shard_map/ppermute | solution.py:39
  74.8 34.3 %collective-permute-start.6 = (bf16[1,512,1024]{2,1,0:T(8,128)(2,1)}, bf16[1,512,1024]{2,1,0:T(8,128)(2,1)}, u32[]{:S(2)}, u32[]{:S(2)}) collective-permute-start(bf16[1,512,1024]{2,1,0:T(8,128)(2,1)} %bitcast.205), channel_id=1, source_target_pairs={{0,8},{1,9},{2,10},{3,11},{4,12},{5,13},{6,14},{7,15},{8,0},{9,1},... | collective-permute-start | bytes 3145736 | tf_op jit(solution)/shard_map/ppermute | solution.py:39
  88.3 25.2 %collective-permute-start.5 = (bf16[2,2,2,2,64,1024]{5,4,3,2,1,0:T(8,128)(2,1)}, bf16[2,2,2,2,64,1024]{5,4,3,2,1,0:T(8,128)(2,1)}, u32[]{:S(2)}, u32[]{:S(2)}) collective-permute-start(bf16[2,2,2,2,64,1024]{5,4,3,2,1,0:T(8,128)(2,1)} %bitcast.190), channel_id=1, source_target_pairs={{0,2},{1,3},{2,0},{3,1},{4,6},{5,7},{6,4},{7,5},{8,10},{9,11},{10,... | collective-permute-start | bytes 6291464 | tf_op jit(solution)/shard_map/ppermute | solution.py:39
  102.6 74.8 %collective-permute-start.14 = (bf16[1,256,4096]{2,1,0:T(8,128)(2,1)}, bf16[1,256,4096]{2,1,0:T(8,128)(2,1)}, u32[]{:S(2)}, u32[]{:S(2)}) collective-permute-start(bf16[1,256,4096]{2,1,0:T(8,128)(2,1)} %bitcast.45.refs_3_), channel_id=1, source_target_pairs={{0,1},{1,0},{2,3},{3,2},{4,5},{5,4},{6,7},{7,6},{8,9},{9,8},{10,11... | collective-permute-start | bytes 6291464 | tf_op jit(solution)/shard_map/ppermute | solution.py:39
  111.9 65.8 %collective-permute-start.11 = (bf16[1,1024,1024]{2,1,0:T(8,128)(2,1)}, bf16[1,1024,1024]{2,1,0:T(8,128)(2,1)}, u32[]{:S(2)}, u32[]{:S(2)}) collective-permute-start(bf16[1,1024,1024]{2,1,0:T(8,128)(2,1)} %bitcast.140), channel_id=1, source_target_pairs={{0,4},{1,5},{2,6},{3,7},{4,0},{5,1},{6,2},{7,3},{8,12},{9,13},{10,... | collective-permute-start | bytes 6291464 | tf_op jit(solution)/shard_map/ppermute | solution.py:39
  113.4 73.1 %collective-permute-start.10 = (bf16[4,256,1024]{2,1,0:T(8,128)(2,1)}, bf16[4,256,1024]{2,1,0:T(8,128)(2,1)}, u32[]{:S(2)}, u32[]{:S(2)}) collective-permute-start(bf16[4,256,1024]{2,1,0:T(8,128)(2,1)} %bitcast.141), channel_id=1, source_target_pairs={{0,2},{1,3},{2,0},{3,1},{4,6},{5,7},{6,4},{7,5},{8,10},{9,11},{10,... | collective-permute-start | bytes 6291464 | tf_op jit(solution)/shard_map/ppermute | solution.py:39
  142.7 43.8 %collective-permute-start.13 = (bf16[256,4096]{1,0:T(8,128)(2,1)}, bf16[256,4096]{1,0:T(8,128)(2,1)}, u32[]{:S(2)}, u32[]{:S(2)}) collective-permute-start(bf16[256,4096]{1,0:T(8,128)(2,1)} %bitcast.63.down_p_own), channel_id=1, source_target_pairs={{0,2},{1,3},{2,0},{3,1},{4,6},{5,7},{6,4},{7,5},{8,10},{9,11},{10,... | collective-permute-start | bytes 6291464 | tf_op jit(solution)/shard_map/ppermute | solution.py:39
  143.0 198.0 %collective-permute-start.25 = (bf16[2,2,2,64,1024]{4,3,2,1,0:T(8,128)(2,1)}, bf16[2,2,2,64,1024]{4,3,2,1,0:T(8,128)(2,1)}, u32[]{:S(2)}, u32[]{:S(2)}) collective-permute-start(bf16[2,2,2,64,1024]{4,3,2,1,0:T(8,128)(2,1)} %combine.9.refs_2_), channel_id=1, source_target_pairs={{0,8},{1,9},{2,10},{3,11},{4,12},{5,13},{6,14},{7,15},{8,0},{9,1},... | collective-permute-start | bytes 3145736 | tf_op jit(solution)/shard_map/ppermute | solution.py:39
  243.4 56.2 %collective-permute-start.20 = (bf16[2,2,2,1024,128]{4,3,2,1,0:T(8,128)(2,1)}, bf16[2,2,2,1024,128]{4,3,2,1,0:T(8,128)(2,1)}, u32[]{:S(2)}, u32[]{:S(2)}) collective-permute-start(bf16[2,2,2,1024,128]{4,3,2,1,0:T(8,128)(2,1)} %combine.10.refs_3_), channel_id=1, source_target_pairs={{0,1},{1,0},{2,3},{3,2},{4,5},{5,4},{6,7},{7,6},{8,9},{9,8},{10,11... | collective-permute-start | bytes 6291464 | tf_op jit(solution)/shard_map/ppermute | solution.py:39
  253.8 52.5 %collective-permute-start.19 = (bf16[2,2,2,32,4096]{4,3,2,1,0:T(8,128)(2,1)}, bf16[2,2,2,32,4096]{4,3,2,1,0:T(8,128)(2,1)}, u32[]{:S(2)}, u32[]{:S(2)}) collective-permute-start(bf16[2,2,2,32,4096]{4,3,2,1,0:T(8,128)(2,1)} %combine.11.refs_12_), channel_id=1, source_target_pairs={{0,4},{1,5},{2,6},{3,7},{4,0},{5,1},{6,2},{7,3},{8,12},{9,13},{10,... | collective-permute-start | bytes 6291464 | tf_op jit(solution)/shard_map/ppermute | solution.py:39
  299.6 45.9 %collective-permute-start.24 = (bf16[512,1024]{1,0:T(8,128)(2,1)}, bf16[512,1024]{1,0:T(8,128)(2,1)}, u32[]{:S(2)}, u32[]{:S(2)}) collective-permute-start(bf16[512,1024]{1,0:T(8,128)(2,1)} %far_back.1.refs_4_), channel_id=1, source_target_pairs={{0,1},{1,0},{2,3},{3,2},{4,5},{5,4},{6,7},{7,6},{8,9},{9,8},{10,11... | collective-permute-start | bytes 3145736 | tf_op jit(solution)/shard_map/ppermute | solution.py:39
  304.7 28.0 %collective-permute-start.22 = (bf16[2,2,1024,128]{3,2,1,0:T(8,128)(2,1)}, bf16[2,2,1024,128]{3,2,1,0:T(8,128)(2,1)}, u32[]{:S(2)}, u32[]{:S(2)}) collective-permute-start(bf16[2,2,1024,128]{3,2,1,0:T(8,128)(2,1)} %get-tuple-element.142.refs_4_), channel_id=1, source_target_pairs={{0,4},{1,5},{2,6},{3,7},{4,0},{5,1},{6,2},{7,3},{8,12},{9,13},{10,... | collective-permute-start | bytes 3145736 | tf_op jit(solution)/shard_map/ppermute | solution.py:39
  311.4 50.7 %collective-permute-start.28 = (bf16[2,2,32,4096]{3,2,1,0:T(8,128)(2,1)}, bf16[2,2,32,4096]{3,2,1,0:T(8,128)(2,1)}, u32[]{:S(2)}, u32[]{:S(2)}) collective-permute-start(bf16[2,2,32,4096]{3,2,1,0:T(8,128)(2,1)} %get-tuple-element.143.refs_3_), channel_id=1, source_target_pairs={{0,1},{1,0},{2,3},{3,2},{4,5},{5,4},{6,7},{7,6},{8,9},{9,8},{10,11... | collective-permute-start | bytes 3145736 | tf_op jit(solution)/shard_map/ppermute | solution.py:39
  317.3 44.7 %collective-permute-start.27 = (bf16[2,2,2,64,1024]{4,3,2,1,0:T(8,128)(2,1)}, bf16[2,2,2,64,1024]{4,3,2,1,0:T(8,128)(2,1)}, u32[]{:S(2)}, u32[]{:S(2)}) collective-permute-start(bf16[2,2,2,64,1024]{4,3,2,1,0:T(8,128)(2,1)} %combine.14.refs_15_), channel_id=1, source_target_pairs={{0,4},{1,5},{2,6},{3,7},{4,0},{5,1},{6,2},{7,3},{8,12},{9,13},{10,... | collective-permute-start | bytes 3145736 | tf_op jit(solution)/shard_map/ppermute | solution.py:39
  341.0 30.9 %collective-permute-start.23 = (bf16[2,2,2,64,1024]{4,3,2,1,0:T(8,128)(2,1)}, bf16[2,2,2,64,1024]{4,3,2,1,0:T(8,128)(2,1)}, u32[]{:S(2)}, u32[]{:S(2)}) collective-permute-start(bf16[2,2,2,64,1024]{4,3,2,1,0:T(8,128)(2,1)} %combine.16.refs_4_), channel_id=1, source_target_pairs={{0,1},{1,0},{2,3},{3,2},{4,5},{5,4},{6,7},{7,6},{8,9},{9,8},{10,11... | collective-permute-start | bytes 3145736 | tf_op jit(solution)/shard_map/ppermute | solution.py:39
  345.4 44.5 %collective-permute-start.35 = (bf16[2,2,64,1024]{3,2,1,0:T(8,128)(2,1)}, bf16[2,2,64,1024]{3,2,1,0:T(8,128)(2,1)}, u32[]{:S(2)}, u32[]{:S(2)}) collective-permute-start(bf16[2,2,64,1024]{3,2,1,0:T(8,128)(2,1)} %get-tuple-element.149.refs_13_), channel_id=1, source_target_pairs={{0,16},{1,17},{2,18},{3,19},{4,20},{5,21},{6,22},{7,23},{8,24},{9,... | collective-permute-start | bytes 1572872 | tf_op jit(solution)/shard_map/ppermute | solution.py:39
  (63 other events, 622.5 us)
Sparse Core Ops, SparseCore 0:
  10.9 107.4 all-gather.3
  121.4 56.9 all-gather.5
  181.9 64.3 all-gather.7
where the time goes:
time: 459 us; the launch traced here: 455 us
  Pallas kernels  280 us (61%)
  waiting for transfers between devices  69.8 us (15%)
  starting transfers between devices  46.7 us (10%)
  local copies, waits for them, and re-layouts  25.7 us (6%)
  other arithmetic  18.8 us (4%)
  between operations  14.5 us (3%)
    pallas_call x25, Pallas kernels, ordered_call(): pl.pallas_call(body, in_specs=list(in_specs) + [pl.BlockSpec(memory_space...  172 us
    ppermute x46, waiting for transfers between devices, swap(): return lax.ppermute(value, BOTH, [(i, i ^ 1 << bit) for i in range(count)])  69.1 us
    ppermute x46, starting transfers between devices, swap(): return lax.ppermute(value, BOTH, [(i, i ^ 1 << bit) for i in range(count)])  46.6 us
    pallas_call x1, Pallas kernels, feed_forward(): pl.pallas_call(feed_kernel, grid_spec=pltpu.PrefetchScalarGridSpec(num_sc...  41.2 us
    pallas_call x9, Pallas kernels, combined(): pl.pallas_call(kernel, grid_spec=pltpu.PrefetchScalarGridSpec(num_scalar_...  34.5 us
    pallas_call x9, Pallas kernels, round_of(): pl.pallas_call(lambda *refs: round_kernel(plans, *refs), grid_spec=pltpu....  31.5 us
    unnamed x80, local copies, waits for them, and re-layouts  14.8 us
  transfers between devices with their start and end apart: 49, of which 10 were waited for; matrix products, arithmetic and copies ran while one was open for 6% of the time, Pallas kernels for 60%

commit v1 on v0

--- a/solution.py
+++ b/solution.py
@@ -1303,14 +1303,14 @@
     )
     last = round_of([value_sum, down_sum, up_sum], (grad_in,))
     last = round_of([key_sum, gain_sum], (last,))
-    last = round_of([value_sum, down_sum, compress_sum], (last,))
+    compressed, layer_out = outputs(
+        before, even, window_mask.reshape(-1, 1), middle, branch, live, compress_in, (last,)
+    )
+    last = round_of([value_sum, down_sum, compress_sum], (compressed,))
     last = round_of([key_sum, gain_sum, up_sum], (last,))
     last = round_of([value_sum, compress_sum], (last,))
     last = round_of([key_sum, down_sum, gain_sum], (last,))
-    compressed, layer_out = outputs(
-        before, even, window_mask.reshape(-1, 1), middle, branch, live, compress_in, (last,)
-    )
-    last = round_of([value_sum, compress_sum], (compressed,))
+    last = round_of([value_sum, compress_sum], (last,))
     last = round_of([key_sum, gain_sum], (last,))
     round_of([gain_sum], (last,))
     grad_value, grad_out = jnp.split(value_sum.total, 2)

time: 459 us -> 452 us (0.985)
  waiting for transfers between devices: 69.8 us -> 61.4 us
    ppermute x46, waiting for transfers between devices: 69.1 us -> 60.8 us  [swap(): return lax.ppermute(value, BOTH, [(i, i ^ 1 << bit) for i in range(count)])]
    unnamed x80 -> x82, local copies, waits for them, and re-layouts: 14.8 us -> 14.6 us
  transfers between devices with their start and end apart: 49 -> 49, of which waited for: 10 -> 9; matrix products, arithmetic and copies ran while one was open for 6% -> 6% of each run, Pallas kernels for 60% -> 61%
where the time goes in v1:
time: 452 us; the launch traced here: 448 us
  Pallas kernels  280 us (62%)
  waiting for transfers between devices  61.4 us (14%)
  starting transfers between devices  48.3 us (11%)
  local copies, waits for them, and re-layouts  25.5 us (6%)
  other arithmetic  18.7 us (4%)
  between operations  14.4 us (3%)
    pallas_call x25, Pallas kernels, ordered_call(): pl.pallas_call(body, in_specs=list(in_specs) + [pl.BlockSpec(memory_space...  172 us
    ppermute x46, waiting for transfers between devices, swap(): return lax.ppermute(value, BOTH, [(i, i ^ 1 << bit) for i in range(count)])  60.8 us
    ppermute x46, starting transfers between devices, swap(): return lax.ppermute(value, BOTH, [(i, i ^ 1 << bit) for i in range(count)])  48.1 us
    pallas_call x1, Pallas kernels, feed_forward(): pl.pallas_call(feed_kernel, grid_spec=pltpu.PrefetchScalarGridSpec(num_sc...  41.2 us
    pallas_call x9, Pallas kernels, combined(): pl.pallas_call(kernel, grid_spec=pltpu.PrefetchScalarGridSpec(num_scalar_...  34.4 us
    pallas_call x9, Pallas kernels, round_of(): pl.pallas_call(lambda *refs: round_kernel(plans, *refs), grid_spec=pltpu....  31.6 us
    unnamed x82, local copies, waits for them, and re-layouts  14.6 us
  transfers between devices with their start and end apart: 49, of which 9 were waited for; matrix products, arithmetic and copies ran while one was open for 6% of the time, Pallas kernels for 61%

profile of v1, /device:TPU:0, one launch (start us, length us, event | category | flops | bytes accessed | tf_op | source)
XLA Modules:
  0.0 447.9 jit_solution(10476003206005928874)
XLA Ops:
  37.7 25.3 %collective-permute-done.4 = bf16[1,64,4096]{2,1,0:T(8,128)(2,1)S(1)} collective-permute-done((bf16[1,64,4096]{2,1,0:T(8,128)(2,1)}, bf16[1,64,4096]{2,1,0:T(8,128)(2,1)S(1)}, u32[]{:S(2)}, u32[]{:S(2)}) %collective-permute-start.4) | collective-permute-done | bytes 524320 | tf_op jit(solution)/shard_map/ppermute | solution.py:39
  83.8 4.2 weight_grads.3
  88.0 11.9 %collective-permute-done.7 = bf16[1,128,4096]{2,1,0:T(8,128)(2,1)} collective-permute-done((bf16[1,128,4096]{2,1,0:T(8,128)(2,1)}, bf16[1,128,4096]{2,1,0:T(8,128)(2,1)}, u32[]{:S(2)}, u32[]{:S(2)}) %collective-permute-start.7) | collective-permute-done | bytes 1048608 | tf_op jit(solution)/shard_map/ppermute | solution.py:39
  103.4 5.6 %collective-permute-done.6 = bf16[1,512,1024]{2,1,0:T(8,128)(2,1)} collective-permute-done((bf16[1,512,1024]{2,1,0:T(8,128)(2,1)}, bf16[1,512,1024]{2,1,0:T(8,128)(2,1)}, u32[]{:S(2)}, u32[]{:S(2)}) %collective-permute-start.6) | collective-permute-done | bytes 1048608 | tf_op jit(solution)/shard_map/ppermute | solution.py:39
  123.7 15.6 %project.2 = (bf16[3,512,1024]{2,1,0:T(8,128)(2,1)}, bf16[3,512,1024]{2,1,0:T(8,128)(2,1)}, bf16[512,1024]{1,0:T(8,128)(2,1)}) custom-call(bf16[512,1024]{1,0:T(8,128)(2,1)} %bitcast.193, bf16[512,1024]{1,0:T(8,128)(2,1)} %bitcast.197, bf16[512,1024]{1,0:T(8,128)(2,1)} %get-tuple-element.113.refs_2_.refs_10_.refs_14_, ...), custom_call_target="tpu_custom_call" | custom-call | flops 99999997952 | bytes 1048576 | tf_op jit(solution)/shard_map/project/pallas_call | solution.py:52
  142.9 13.2 %project.3 = (bf16[3,512,1024]{2,1,0:T(8,128)(2,1)}, bf16[3,512,1024]{2,1,0:T(8,128)(2,1)}) custom-call(bf16[512,1024]{1,0:T(8,128)(2,1)} %collective-permute-done.8.refs_0_.refs_11_, bf16[512,1024]{1,0:T(8,128)(2,1)} %collective-permute-done.9.refs_1_.refs_12_, bf16[512,1024]{1,0:T(8,128)(2,1)} %get-tuple-element.115.refs_2_.refs_13_, ...), custom_call_target="tpu_custom_call" | custom-call | flops 99999997952 | bytes 1048576 | tf_op jit(solution)/shard_map/project/pallas_call | solution.py:52
  156.2 19.6 %attend.1 = (bf16[512,1024]{1,0:T(8,128)(2,1)}, bf16[2,8,768,256]{3,2,1,0:T(8,128)(2,1)}, bf16[2,8,768,256]{3,2,1,0:T(8,128)(2,1)}) custom-call(s32[1]{0:T(128)} %bitcast.53.refs_0_, bf16[512,1024]{1,0:T(8,128)(2,1)} %get-tuple-element.114.refs_2_.refs_1_, bf16[3,512,1024]{2,1,0:T(8,128)(2,1)} %get-tuple-element.118.refs_2_, ...), custom_call_target="tpu_custom_call" | custom-call | flops 99999997952 | bytes 1048576 | tf_op jit(solution)/shard_map/attend/pallas_call | solution.py:52
  179.1 5.0 %join.1 = (f32[512,1024]{1,0:T(8,128)}, bf16[512,1024]{1,0:T(8,128)(2,1)}) custom-call(bf16[512,1024]{1,0:T(8,128)(2,1)} %get-tuple-element.122.refs_1_.refs_0_.refs_14_, bf16[512,1024]{1,0:T(8,128)(2,1)} %bitcast.203, f32[1,1024]{1,0:T(1,128)} %slice.76.refs_2_.refs_4_, bf16[32,2,16,1024]{3,2,1,0:T(8,128)(2,1)} %all-gather.6.cloned.1.call-done.refs_3_.refs_5_, ...), custom_call_target="tpu_custom_call" | custom-call | flops 99999997952 | bytes 1048576 | tf_op jit(solution)/shard_map/join/pallas_call | solution.py:52
  187.8 41.2 %feed_forward.1 = (f32[512,1024]{1,0:T(8,128)}, f32[512,1024]{1,0:T(8,128)}, bf16[8,2,1024,128]{3,2,1,0:T(8,128)(2,1)}, bf16[8,2,1024,128]{3,2,1,0:T(8,128)(2,1)...) custom-call(s32[3]{0:T(128)} %pad_add_fusion.mine, bf16[512,1024]{1,0:T(8,128)(2,1)} %get-tuple-element.124.ffn, ...), custom_call_target="tpu_custom_call" | custom-call | flops 99999997952 | bytes 1048576 | tf_op jit(solution)/shard_map/feed_forward/pallas_call | solution.py:540
  229.6 7.4 %part.1 = (f32[512,1024]{1,0:T(8,128)}, bf16[512,1024]{1,0:T(8,128)(2,1)}, bf16[512,1024]{1,0:T(8,128)(2,1)}, f32[1,1024]{1,0:T(1,128)}) custom-call(f32[512,1024]{1,0:T(8,128)} %get-tuple-element.126.refs_0_, f32[512,1024]{1,0:T(8,128)} %get-tuple-element.123.refs_1_.refs_3_, bf16[512,1024]{1,0:T(8,128)(2,1)} %bitcast.150, f32[512,1]{1,0:T(8,128)} %bitcast.164, ...), custom_call_target="tpu_custom_call" | custom-call | flops 99999997952 | bytes 1048576 | tf_op jit(solution)/shard_map/part/pallas_call | solution.py:52
  238.3 5.1 %combine.10.refs_3_ = bf16[2,2,2,1024,128]{4,3,2,1,0:T(8,128)(2,1)} custom-call(s32[5]{0:T(128)} %copy-done, bf16[2,2,2,2,1024,128]{5,4,3,2,1,0:T(8,128)(2,1)} %bitcast.222, bf16[2,2,2,2,1024,128]{5,4,3,2,1,0:T(8,128)(2,1)} %collective-permute-done.17.refs_2_, bf16[512,1024]{1,0:T(8,128)(2,1)} %get-tuple-element.127.refs_3_.refs_0_), custom_call_target="tpu_custom_call" | custom-call | flops 99999997952 | bytes 1048576 | tf_op jit(solution)/shard_map/combine/pallas_call | solution.py:189
  243.3 5.3 %collective-permute-start.20 = (bf16[2,2,2,1024,128]{4,3,2,1,0:T(8,128)(2,1)}, bf16[2,2,2,1024,128]{4,3,2,1,0:T(8,128)(2,1)}, u32[]{:S(2)}, u32[]{:S(2)}) collective-permute-start(bf16[2,2,2,1024,128]{4,3,2,1,0:T(8,128)(2,1)} %combine.10.refs_3_), channel_id=1, source_target_pairs={{0,1},{1,0},{2,3},{3,2},{4,5},{5,4},{6,7},{7,6},{8,9},{9,8},{10,11... | collective-permute-start | bytes 6291464 | tf_op jit(solution)/shard_map/ppermute | solution.py:39
  248.6 5.0 %combine.11.refs_12_ = bf16[2,2,2,32,4096]{4,3,2,1,0:T(8,128)(2,1)} custom-call(s32[5]{0:T(128)} %copy-done, bf16[2,2,2,2,32,4096]{5,4,3,2,1,0:T(8,128)(2,1)} %bitcast.220, bf16[2,2,2,2,32,4096]{5,4,3,2,1,0:T(8,128)(2,1)} %collective-permute-done.16.refs_2_, bf16[2,2,2,1024,128]{4,3,2,1,0:T(8,128)(2,1)} %combine.10.refs_3_), custom_call_target="tpu_custom_call" | custom-call | flops 99999997952 | bytes 1048576 | tf_op jit(solution)/shard_map/combine/pallas_call | solution.py:189
  254.2 23.7 %attend_back.1 = (bf16[512,1024]{1,0:T(8,128)(2,1)}, bf16[3,512,1024]{2,1,0:T(8,128)(2,1)}, bf16[3,512,1024]{2,1,0:T(8,128)(2,1)}, bf16[3,512,1024]{2,1,0:T(8,128)(2,1)}, bf16[3,512,1024]{2,1,0:T(8,128)(2,1)}) custom-call(bf16[512,1024]{1,0:T(8,128)(2,1)} %get-tuple-element.127.refs_3_.refs_0_, bf16[512,1024]{1,0:T(8,128)(2,1)} %get-tuple-element.114.refs_2_.refs_1_, ...), custom_call_target="tpu_custom_call" | custom-call | flops 99999997952 | bytes 1048576 | tf_op jit(solution)/shard_map/attend_back/pallas_call | solution.py:52
  277.9 14.0 %weight_grads.4 = (bf16[8,2,64,1024]{3,2,1,0:T(8,128)(2,1)}, bf16[8,2,64,1024]{3,2,1,0:T(8,128)(2,1)}) custom-call(s32[1]{0:T(128)} %bitcast.10.refs_0_, bf16[3,512,1024]{2,1,0:T(8,128)(2,1)} %get-tuple-element.137.refs_1_.refs_2_.refs_3_, bf16[3,512,1024]{2,1,0:T(8,128)(2,1)} %get-tuple-element.137.refs_1_.refs_2_.refs_3_, ...), custom_call_target="tpu_custom_call" | custom-call | flops 99999997952 | bytes 1048576 | tf_op jit(solution)/shard_map/weight_grads/pallas_call | solution.py:52
  292.0 7.5 %far_back.1.refs_4_ = bf16[512,1024]{1,0:T(8,128)(2,1)} custom-call(s32[1]{0:T(128)} %bitcast.53.refs_0_, bf16[3,512,1024]{2,1,0:T(8,128)(2,1)} %get-tuple-element.135.refs_1_.refs_4_.refs_5_.refs_6_, bf16[3,512,1024]{2,1,0:T(8,128)(2,1)} %get-tuple-element.138.refs_4_.refs_5_.refs_6_.refs_2_, bf16[2,128,1024]{2,1,0:T(8,128)(2,1)} %fusion.refs_3_, ...), custom_call_target="tpu_custom_call" | custom-call | flops 99999997952 | bytes 1048576 | tf_op jit(solution)/shard_map/far_back/pallas_call | solution.py:52
  299.6 5.0 %combine.12 = (bf16[2,2,1024,128]{3,2,1,0:T(8,128)(2,1)}, f32[2,2,1024,128]{3,2,1,0:T(8,128)}) custom-call(s32[5]{0:T(128)} %copy-done, bf16[2,2,2,2,1024,128]{5,4,3,2,1,0:T(8,128)(2,1)} %bitcast.223, bf16[2,2,2,2,1024,128]{5,4,3,2,1,0:T(8,128)(2,1)} %collective-permute-done.17.refs_2_, bf16[2,2,2,1024,128]{4,3,2,1,0:T(8,128)(2,1)} %collective-permute-done.20.refs_3_, ...), custom_call_target="tpu_custom_call" | custom-call | flops 99999997952 | bytes 1048576 | tf_op jit(solution)/shard_map/combine/pallas_call | solution.py:189
  306.2 5.0 %combine.13 = (bf16[2,2,32,4096]{3,2,1,0:T(8,128)(2,1)}, f32[2,2,32,4096]{3,2,1,0:T(8,128)}) custom-call(s32[5]{0:T(128)} %copy-done, bf16[2,2,2,2,32,4096]{5,4,3,2,1,0:T(8,128)(2,1)} %bitcast.221, bf16[2,2,2,2,32,4096]{5,4,3,2,1,0:T(8,128)(2,1)} %collective-permute-done.16.refs_2_, bf16[2,2,2,32,4096]{4,3,2,1,0:T(8,128)(2,1)} %collective-permute-done.19.refs_3_, ...), custom_call_target="tpu_custom_call" | custom-call | flops 99999997952 | bytes 1048576 | tf_op jit(solution)/shard_map/combine/pallas_call | solution.py:189
  317.8 14.5 %weight_grads.5 = (bf16[8,2,64,1024]{3,2,1,0:T(8,128)(2,1)}, bf16[8,2,64,1024]{3,2,1,0:T(8,128)(2,1)}) custom-call(s32[1]{0:T(128)} %bitcast.10.refs_0_, bf16[3,512,1024]{2,1,0:T(8,128)(2,1)} %get-tuple-element.134.refs_1_.refs_2_.refs_3_, bf16[3,512,1024]{2,1,0:T(8,128)(2,1)} %get-tuple-element.134.refs_1_.refs_2_.refs_3_, ...), custom_call_target="tpu_custom_call" | custom-call | flops 99999997952 | bytes 1048576 | tf_op jit(solution)/shard_map/weight_grads/pallas_call | solution.py:52
  348.8 12.0 %finish.1 = (bf16[512,1024]{1,0:T(8,128)(2,1)}, f32[1,1024]{1,0:T(1,128)}) custom-call(bf16[512,1024]{1,0:T(8,128)(2,1)} %get-tuple-element.136.refs_0_, bf16[3,512,1024]{2,1,0:T(8,128)(2,1)} %get-tuple-element.134.refs_1_.refs_2_.refs_3_, bf16[3,512,1024]{2,1,0:T(8,128)(2,1)} %get-tuple-element.137.refs_1_.refs_2_.refs_3_, ...), custom_call_target="tpu_custom_call" | custom-call | flops 99999997952 | bytes 1048576 | tf_op jit(solution)/shard_map/finish/pallas_call | solution.py:52
  361.9 6.4 %round.9 = (bf16[2,2,64,1024]{3,2,1,0:T(8,128)(2,1)}, f32[2,2,64,1024]{3,2,1,0:T(8,128)}, bf16[2,32,4096]{2,1,0:T(8,128)(2,1)}, f32[2,32,4096]{2,1,0:T(8,128)}, ...) custom-call(s32[5]{0:T(128)} %copy-done, bf16[2,2,2,2,64,1024]{5,4,3,2,1,0:T(8,128)(2,1)} %bitcast.146, ...), custom_call_target="tpu_custom_call" | custom-call | flops 99999997952 | bytes 1048576 | tf_op jit(solution)/shard_map/round/pallas_call | solution.py:246
  376.7 7.2 %outputs.1 = (bf16[256,1024]{1,0:T(8,128)(2,1)}, bf16[512,1024]{1,0:T(8,128)(2,1)}) custom-call(bf16[256,1024]{1,0:T(8,128)(2,1)} %bitcast.152, bf16[256,1024]{1,0:T(8,128)(2,1)} %get-tuple-element.117.refs_1_, f32[256,1]{1,0:T(8,128)} %copy.54.refs_2_, f32[512,1024]{1,0:T(8,128)} %get-tuple-element.123.refs_1_.refs_3_, ...), custom_call_target="tpu_custom_call" | custom-call | flops 99999997952 | bytes 1048576 | tf_op jit(solution)/shard_map/outputs/pallas_call | solution.py:52
  389.9 4.5 %round.11 = (bf16[2,64,1024]{2,1,0:T(8,128)(2,1)}, f32[2,64,1024]{2,1,0:T(8,128)}, bf16[32,4096]{1,0:T(8,128)(2,1)}, f32[32,4096]{1,0:T(8,128)}, bf16[2,64,1024]{2,1,0:T(8,128)(2,1)}, /*index=5*/f32[2,64,1024]{2,1,0:T(8,128)}) custom-call(s32[5]{0:T(128)} %copy-done, f32[2,2,64,1024]{3,2,1,0:T(8,128)} %get-tuple-element.163.refs_1_, ...), custom_call_target="tpu_custom_call" | custom-call | flops 99999997952 | bytes 1048576 | tf_op jit(solution)/shard_map/round/pallas_call | solution.py:246
  403.5 5.7 %collective-permute-done.39.refs_2_ = bf16[2,64,1024]{2,1,0:T(8,128)(2,1)S(1)} collective-permute-done((bf16[2,64,1024]{2,1,0:T(8,128)(2,1)}, bf16[2,64,1024]{2,1,0:T(8,128)(2,1)S(1)}, u32[]{:S(2)}, u32[]{:S(2)}) %collective-permute-start.39) | collective-permute-done | bytes 262176 | tf_op jit(solution)/shard_map/ppermute | solution.py:39
  (247 shorter events, 163.4 us)
Async XLA Ops:
  7.2 111.1 %all-gather.4.cloned.1.call-start = ((), (), s32[]{:S(2)}) async-start(), calls=%async_computation | async-start | bytes 7569408 | tf_op jit(solution)/shard_map/all_gather | solution.py:1146
  9.7 169.4 %all-gather.6.cloned.1.call-start = ((), (), s32[]{:S(2)}) async-start(), calls=%async_computation.1 | async-start | bytes 2162688 | tf_op jit(solution)/shard_map/all_gather | solution.py:1146
  16.5 62.4 %collective-permute-start = (bf16[512,1024]{1,0:T(8,128)(2,1)}, bf16[512,1024]{1,0:T(8,128)(2,1)}, u32[]{:S(2)}, u32[]{:S(2)}) collective-permute-start(bf16[512,1024]{1,0:T(8,128)(2,1)} %bitcast.200), channel_id=1, source_target_pairs={{0,1},{1,0},{2,3},{3,2},{4,5},{5,4},{6,7},{7,6},{8,9},{9,8},{10,11... | collective-permute-start | bytes 3145736 | tf_op jit(solution)/shard_map/ppermute | solution.py:39
  17.0 125.7 %collective-permute-start.8 = (bf16[512,1024]{1,0:T(8,128)(2,1)}, bf16[512,1024]{1,0:T(8,128)(2,1)}, u32[]{:S(2)}, u32[]{:S(2)}) collective-permute-start(bf16[512,1024]{1,0:T(8,128)(2,1)} %bitcast.192), channel_id=1, source_target_pairs={{0,1},{1,0},{2,3},{3,2},{4,5},{5,4},{6,7},{7,6},{8,9},{9,8},{10,11... | collective-permute-start | bytes 3145736 | tf_op jit(solution)/shard_map/ppermute | solution.py:39
  18.5 124.4 %collective-permute-start.9 = (bf16[512,1024]{1,0:T(8,128)(2,1)}, bf16[512,1024]{1,0:T(8,128)(2,1)}, u32[]{:S(2)}, u32[]{:S(2)}) collective-permute-start(bf16[512,1024]{1,0:T(8,128)(2,1)} %bitcast.196), channel_id=1, source_target_pairs={{0,1},{1,0},{2,3},{3,2},{4,5},{5,4},{6,7},{7,6},{8,9},{9,8},{10,11... | collective-permute-start | bytes 3145736 | tf_op jit(solution)/shard_map/ppermute | solution.py:39
  19.1 272.9 %all-gather.8.cloned.1.call-start = ((), (), s32[]{:S(2)}) async-start(), calls=%async_computation.2 | async-start | bytes 4325376 | tf_op jit(solution)/shard_map/all_gather | solution.py:1146
  33.9 29.1 %collective-permute-start.4 = (bf16[1,64,4096]{2,1,0:T(8,128)(2,1)}, bf16[1,64,4096]{2,1,0:T(8,128)(2,1)S(1)}, u32[]{:S(2)}, u32[]{:S(2)}) collective-permute-start(bf16[1,64,4096]{2,1,0:T(8,128)(2,1)} %bitcast.214), channel_id=1, source_target_pairs={{0,8},{1,9},{2,10},{3,11},{4,12},{5,13},{6,14},{7,15},{8,0},{9,1},... | collective-permute-start | bytes 1572872 | tf_op jit(solution)/shard_map/ppermute | solution.py:39
  37.3 34.3 %collective-permute-start.3 = (bf16[1,256,1024]{2,1,0:T(8,128)(2,1)}, bf16[1,256,1024]{2,1,0:T(8,128)(2,1)S(1)}, u32[]{:S(2)}, u32[]{:S(2)}) collective-permute-start(bf16[1,256,1024]{2,1,0:T(8,128)(2,1)} %bitcast.211), channel_id=1, source_target_pairs={{0,16},{1,17},{2,18},{3,19},{4,20},{5,21},{6,22},{7,23},{8,24},{9,... | collective-permute-start | bytes 1572872 | tf_op jit(solution)/shard_map/ppermute | solution.py:39
  66.0 34.0 %collective-permute-start.7 = (bf16[1,128,4096]{2,1,0:T(8,128)(2,1)}, bf16[1,128,4096]{2,1,0:T(8,128)(2,1)}, u32[]{:S(2)}, u32[]{:S(2)}) collective-permute-start(bf16[1,128,4096]{2,1,0:T(8,128)(2,1)} %bitcast.208), channel_id=1, source_target_pairs={{0,4},{1,5},{2,6},{3,7},{4,0},{5,1},{6,2},{7,3},{8,12},{9,13},{10,... | collective-permute-start | bytes 3145736 | tf_op jit(solution)/shard_map/ppermute | solution.py:39
  74.6 34.4 %collective-permute-start.6 = (bf16[1,512,1024]{2,1,0:T(8,128)(2,1)}, bf16[1,512,1024]{2,1,0:T(8,128)(2,1)}, u32[]{:S(2)}, u32[]{:S(2)}) collective-permute-start(bf16[1,512,1024]{2,1,0:T(8,128)(2,1)} %bitcast.205), channel_id=1, source_target_pairs={{0,8},{1,9},{2,10},{3,11},{4,12},{5,13},{6,14},{7,15},{8,0},{9,1},... | collective-permute-start | bytes 3145736 | tf_op jit(solution)/shard_map/ppermute | solution.py:39
  88.0 25.4 %collective-permute-start.5 = (bf16[2,2,2,2,64,1024]{5,4,3,2,1,0:T(8,128)(2,1)}, bf16[2,2,2,2,64,1024]{5,4,3,2,1,0:T(8,128)(2,1)}, u32[]{:S(2)}, u32[]{:S(2)}) collective-permute-start(bf16[2,2,2,2,64,1024]{5,4,3,2,1,0:T(8,128)(2,1)} %bitcast.190), channel_id=1, source_target_pairs={{0,2},{1,3},{2,0},{3,1},{4,6},{5,7},{6,4},{7,5},{8,10},{9,11},{10,... | collective-permute-start | bytes 6291464 | tf_op jit(solution)/shard_map/ppermute | solution.py:39
  102.5 74.8 %collective-permute-start.14 = (bf16[1,256,4096]{2,1,0:T(8,128)(2,1)}, bf16[1,256,4096]{2,1,0:T(8,128)(2,1)}, u32[]{:S(2)}, u32[]{:S(2)}) collective-permute-start(bf16[1,256,4096]{2,1,0:T(8,128)(2,1)} %bitcast.45.refs_3_), channel_id=1, source_target_pairs={{0,1},{1,0},{2,3},{3,2},{4,5},{5,4},{6,7},{7,6},{8,9},{9,8},{10,11... | collective-permute-start | bytes 6291464 | tf_op jit(solution)/shard_map/ppermute | solution.py:39
  111.8 65.8 %collective-permute-start.11 = (bf16[1,1024,1024]{2,1,0:T(8,128)(2,1)}, bf16[1,1024,1024]{2,1,0:T(8,128)(2,1)}, u32[]{:S(2)}, u32[]{:S(2)}) collective-permute-start(bf16[1,1024,1024]{2,1,0:T(8,128)(2,1)} %bitcast.140), channel_id=1, source_target_pairs={{0,4},{1,5},{2,6},{3,7},{4,0},{5,1},{6,2},{7,3},{8,12},{9,13},{10,... | collective-permute-start | bytes 6291464 | tf_op jit(solution)/shard_map/ppermute | solution.py:39
  113.4 73.1 %collective-permute-start.10 = (bf16[4,256,1024]{2,1,0:T(8,128)(2,1)}, bf16[4,256,1024]{2,1,0:T(8,128)(2,1)}, u32[]{:S(2)}, u32[]{:S(2)}) collective-permute-start(bf16[4,256,1024]{2,1,0:T(8,128)(2,1)} %bitcast.141), channel_id=1, source_target_pairs={{0,2},{1,3},{2,0},{3,1},{4,6},{5,7},{6,4},{7,5},{8,10},{9,11},{10,... | collective-permute-start | bytes 6291464 | tf_op jit(solution)/shard_map/ppermute | solution.py:39
  142.7 43.8 %collective-permute-start.13 = (bf16[256,4096]{1,0:T(8,128)(2,1)}, bf16[256,4096]{1,0:T(8,128)(2,1)}, u32[]{:S(2)}, u32[]{:S(2)}) collective-permute-start(bf16[256,4096]{1,0:T(8,128)(2,1)} %bitcast.63.down_p_own), channel_id=1, source_target_pairs={{0,2},{1,3},{2,0},{3,1},{4,6},{5,7},{6,4},{7,5},{8,10},{9,11},{10,... | collective-permute-start | bytes 6291464 | tf_op jit(solution)/shard_map/ppermute | solution.py:39
  142.9 197.8 %collective-permute-start.25 = (bf16[2,2,2,64,1024]{4,3,2,1,0:T(8,128)(2,1)}, bf16[2,2,2,64,1024]{4,3,2,1,0:T(8,128)(2,1)}, u32[]{:S(2)}, u32[]{:S(2)}) collective-permute-start(bf16[2,2,2,64,1024]{4,3,2,1,0:T(8,128)(2,1)} %combine.9.refs_2_), channel_id=1, source_target_pairs={{0,8},{1,9},{2,10},{3,11},{4,12},{5,13},{6,14},{7,15},{8,0},{9,1},... | collective-permute-start | bytes 3145736 | tf_op jit(solution)/shard_map/ppermute | solution.py:39
  243.3 56.3 %collective-permute-start.20 = (bf16[2,2,2,1024,128]{4,3,2,1,0:T(8,128)(2,1)}, bf16[2,2,2,1024,128]{4,3,2,1,0:T(8,128)(2,1)}, u32[]{:S(2)}, u32[]{:S(2)}) collective-permute-start(bf16[2,2,2,1024,128]{4,3,2,1,0:T(8,128)(2,1)} %combine.10.refs_3_), channel_id=1, source_target_pairs={{0,1},{1,0},{2,3},{3,2},{4,5},{5,4},{6,7},{7,6},{8,9},{9,8},{10,11... | collective-permute-start | bytes 6291464 | tf_op jit(solution)/shard_map/ppermute | solution.py:39
  253.6 52.6 %collective-permute-start.19 = (bf16[2,2,2,32,4096]{4,3,2,1,0:T(8,128)(2,1)}, bf16[2,2,2,32,4096]{4,3,2,1,0:T(8,128)(2,1)}, u32[]{:S(2)}, u32[]{:S(2)}) collective-permute-start(bf16[2,2,2,32,4096]{4,3,2,1,0:T(8,128)(2,1)} %combine.11.refs_12_), channel_id=1, source_target_pairs={{0,4},{1,5},{2,6},{3,7},{4,0},{5,1},{6,2},{7,3},{8,12},{9,13},{10,... | collective-permute-start | bytes 6291464 | tf_op jit(solution)/shard_map/ppermute | solution.py:39
  299.6 45.8 %collective-permute-start.24 = (bf16[512,1024]{1,0:T(8,128)(2,1)}, bf16[512,1024]{1,0:T(8,128)(2,1)}, u32[]{:S(2)}, u32[]{:S(2)}) collective-permute-start(bf16[512,1024]{1,0:T(8,128)(2,1)} %far_back.1.refs_4_), channel_id=1, source_target_pairs={{0,1},{1,0},{2,3},{3,2},{4,5},{5,4},{6,7},{7,6},{8,9},{9,8},{10,11... | collective-permute-start | bytes 3145736 | tf_op jit(solution)/shard_map/ppermute | solution.py:39
  304.6 27.7 %collective-permute-start.22 = (bf16[2,2,1024,128]{3,2,1,0:T(8,128)(2,1)}, bf16[2,2,1024,128]{3,2,1,0:T(8,128)(2,1)}, u32[]{:S(2)}, u32[]{:S(2)}) collective-permute-start(bf16[2,2,1024,128]{3,2,1,0:T(8,128)(2,1)} %get-tuple-element.142.refs_4_), channel_id=1, source_target_pairs={{0,4},{1,5},{2,6},{3,7},{4,0},{5,1},{6,2},{7,3},{8,12},{9,13},{10,... | collective-permute-start | bytes 3145736 | tf_op jit(solution)/shard_map/ppermute | solution.py:39
  311.3 50.6 %collective-permute-start.28 = (bf16[2,2,32,4096]{3,2,1,0:T(8,128)(2,1)}, bf16[2,2,32,4096]{3,2,1,0:T(8,128)(2,1)}, u32[]{:S(2)}, u32[]{:S(2)}) collective-permute-start(bf16[2,2,32,4096]{3,2,1,0:T(8,128)(2,1)} %get-tuple-element.143.refs_3_), channel_id=1, source_target_pairs={{0,1},{1,0},{2,3},{3,2},{4,5},{5,4},{6,7},{7,6},{8,9},{9,8},{10,11... | collective-permute-start | bytes 3145736 | tf_op jit(solution)/shard_map/ppermute | solution.py:39
  317.2 44.6 %collective-permute-start.27 = (bf16[2,2,2,64,1024]{4,3,2,1,0:T(8,128)(2,1)}, bf16[2,2,2,64,1024]{4,3,2,1,0:T(8,128)(2,1)}, u32[]{:S(2)}, u32[]{:S(2)}) collective-permute-start(bf16[2,2,2,64,1024]{4,3,2,1,0:T(8,128)(2,1)} %combine.14.refs_15_), channel_id=1, source_target_pairs={{0,4},{1,5},{2,6},{3,7},{4,0},{5,1},{6,2},{7,3},{8,12},{9,13},{10,... | collective-permute-start | bytes 3145736 | tf_op jit(solution)/shard_map/ppermute | solution.py:39
  340.7 31.0 %collective-permute-start.23 = (bf16[2,2,2,64,1024]{4,3,2,1,0:T(8,128)(2,1)}, bf16[2,2,2,64,1024]{4,3,2,1,0:T(8,128)(2,1)}, u32[]{:S(2)}, u32[]{:S(2)}) collective-permute-start(bf16[2,2,2,64,1024]{4,3,2,1,0:T(8,128)(2,1)} %combine.16.refs_4_), channel_id=1, source_target_pairs={{0,1},{1,0},{2,3},{3,2},{4,5},{5,4},{6,7},{7,6},{8,9},{9,8},{10,11... | collective-permute-start | bytes 3145736 | tf_op jit(solution)/shard_map/ppermute | solution.py:39
  345.4 44.5 %collective-permute-start.35 = (bf16[2,2,64,1024]{3,2,1,0:T(8,128)(2,1)}, bf16[2,2,64,1024]{3,2,1,0:T(8,128)(2,1)}, u32[]{:S(2)}, u32[]{:S(2)}) collective-permute-start(bf16[2,2,64,1024]{3,2,1,0:T(8,128)(2,1)} %get-tuple-element.149.refs_13_), channel_id=1, source_target_pairs={{0,16},{1,17},{2,18},{3,19},{4,20},{5,21},{6,22},{7,23},{8,24},{9,... | collective-permute-start | bytes 1572872 | tf_op jit(solution)/shard_map/ppermute | solution.py:39
  (64 other events, 601.5 us)
Sparse Core Ops, SparseCore 0:
  10.9 107.3 all-gather.3
  121.3 56.9 all-gather.5
  181.9 64.3 all-gather.7
